TPU v7x, 512 devices: a whole 4x8x8 slice. The times are simulated.
512 devices in a mesh: band: 64 (over z, y), lev: 8 (over x, core).
Axes of the slice: x: 4, y: 8, z: 8, core: 2. Of those that a mesh axis runs over, the one named last changes fastest.
Arguments:
- spectra: bfloat16 [2, 64, 320, 641], P(None, 'lev', 'band'), may hold values from -0.15625 to 0.15625
- legendre: bfloat16 [8, 64, 320, 641], P('lev', None, 'band'), may hold values from -0.25 to 0.25
- pairing: int32 [320], P('band'), may hold values from 0 to 319, each once
- eta_shift: bfloat16 [16, 512, 2816], P('lev', 'band'), may hold values from -4 to 4
- cells: int32 [3, 16, 512, 2816], P(None, 'lev', 'band'), may hold values from -1 to 2815, as said below
Outputs:
- advected: bfloat16 [2, 16, 512, 2816], P(None, 'lev', 'band')
- displacement: float32 [2, 16, 512, 2816], P(None, 'lev', 'band')
Inputs may be any that keep to these rules, and one draw needn't show every extreme that they name: cells[0] is the arrival row or the row before it, cells[1] the arrival longitude or the one before it (cyclically), cells[2] the arrival level or the one before it.
All inputs are finite; a program needn't handle non-finite values.
Results may differ from a plain program's by a relative error of at most 0.0076.
Values may be sent and summed in bfloat16 or wider, within the bound.
A program may use at most 64 MiB of HBM per device.

v0:
```python
import math

import jax
import jax.numpy as jnp
from jax import lax
from jax.sharding import PartitionSpec as P

M = 640
ITERS = 2


COURANT = 0.8


def with_halo(array, sides, width):
    for axis, dim in sides:
        size, length = (lax.axis_size(axis), array.shape[dim])
        up = [(i, (i + 1) % size) for i in range(size - 1)]
        down = [(j, i) for i, j in up]
        last = lax.slice_in_dim(array, length - width, length, axis=dim)
        first = lax.slice_in_dim(array, 0, width, axis=dim)
        before = lax.ppermute(last, axis, up)
        after = lax.ppermute(first, axis, down)
        array = jnp.concatenate([before, array, after], axis=dim)
    return array


def cubic_weights(fraction):
    return (
        -fraction * (fraction - 1.0) * (fraction - 2.0) / 6.0,
        (fraction + 1.0) * (fraction - 1.0) * (fraction - 2.0) / 2.0,
        -(fraction + 1.0) * fraction * (fraction - 2.0) / 2.0,
        (fraction + 1.0) * fraction * (fraction - 1.0) / 6.0,
    )


def tap_weights(shift, offset):
    fraction = jnp.clip(-shift - offset.astype(jnp.float32), -0.5, 1.5)
    first, second, third, fourth = cubic_weights(fraction)
    nothing = jnp.zeros_like(fraction)
    at_arrival = offset == 0
    return (
        jnp.where(at_arrival, nothing, first),
        jnp.where(at_arrival, first, second),
        jnp.where(at_arrival, second, third),
        jnp.where(at_arrival, third, fourth),
        jnp.where(at_arrival, fourth, nothing),
    )


def rolled_copies(padded):
    return [jnp.roll(padded, 2 - lon_step, axis=3) for lon_step in range(5)]


def interpolate(copies, field_ids, level_taps, row_taps, lon_taps):
    level_count = level_taps[0].shape[0]
    row_count = level_taps[0].shape[1]
    totals = [jnp.zeros(level_taps[0].shape, jnp.float32) for field_id in field_ids]
    for level_step in range(5):
        for row_step in range(5):
            outer = level_taps[level_step] * row_taps[row_step]
            for position in range(len(field_ids)):
                inner = jnp.zeros(outer.shape, jnp.float32)
                for lon_step in range(5):
                    block = copies[lon_step][
                        level_step : level_step + level_count,
                        field_ids[position],
                        row_step : row_step + row_count,
                        :,
                    ]
                    inner = inner + lon_taps[lon_step] * block.astype(jnp.float32)
                totals[position] = totals[position] + outer * inner
    return totals


def departure(
    fields,
    wind_copies,
    tracer_copies,
    wind_ids,
    tracer_ids,
    eta_shift,
    row_offset,
    lon_offset,
    level_offset,
):
    east = fields[:, 0].astype(jnp.float32)
    north = fields[:, 1].astype(jnp.float32)
    level_taps = tap_weights(eta_shift.astype(jnp.float32), level_offset)
    shift_row = COURANT * north
    shift_lon = COURANT * east
    for sweep in range(ITERS):
        row_taps = tap_weights(shift_row, row_offset)
        lon_taps = tap_weights(shift_lon, lon_offset)
        east_found, north_found = interpolate(wind_copies, wind_ids, level_taps, row_taps, lon_taps)
        shift_row = 0.5 * COURANT * (north + north_found)
        shift_lon = 0.5 * COURANT * (east + east_found)
    row_taps = tap_weights(shift_row, row_offset)
    lon_taps = tap_weights(shift_lon, lon_offset)
    heat, moisture = interpolate(tracer_copies, tracer_ids, level_taps, row_taps, lon_taps)
    return (jnp.stack([heat, moisture]).astype(jnp.bfloat16), jnp.stack([shift_row, shift_lon]))


def split_halves(spectra, pairing):
    width = spectra.shape[-1]
    columns = lax.broadcasted_iota(jnp.int32, (pairing.shape[0], width), 1)
    first_part = columns < (width - 1 - pairing)[:, None]
    nothing = jnp.zeros((), spectra.dtype)
    return jnp.stack(
        [jnp.where(first_part, spectra, nothing), jnp.where(first_part, nothing, spectra)]
    )


def synthesis(pair_ids, lon_ids, lon_total):
    orders = jnp.stack([pair_ids, M - 1 - pair_ids])
    phase = (orders[:, :, None] * lon_ids[None, None, :] % lon_total).astype(jnp.float32) * (
        2.0 * math.pi / lon_total
    )
    weight = jnp.where(orders == 0, 1.0, 2.0).astype(jnp.float32)[:, :, None]
    return jnp.stack([weight * jnp.cos(phase), -weight * jnp.sin(phase)]).astype(jnp.bfloat16)


def legendre_rows(table, halves):
    return jnp.einsum(
        "scpk,hrfpk->cpsfhr", table, halves, preferred_element_type=jnp.float32
    ).astype(jnp.bfloat16)


def per_device(spectra, legendre, pairing, eta_shift, cells):
    grid_shape = eta_shift.shape
    row_count = grid_shape[1]
    halves = split_halves(spectra, pairing)
    result = legendre_rows(lax.all_gather(legendre, "lev", axis=0, tiled=True), halves)
    local_sums = result.reshape(result.shape[0], result.shape[1], -1)
    spectral = lax.all_to_all(local_sums, "band", split_axis=0, concat_axis=1, tiled=True)
    all_pairs = lax.all_gather(pairing, "band", axis=0, tiled=True)
    field_count = 4 * grid_shape[0]
    spectral = spectral.reshape(all_pairs.shape[0], row_count, field_count, 2, 2)
    lon_total = grid_shape[2]
    lon_half = lon_total // 2
    pieces = []
    for lon_part in range(2):
        lon_block = lon_part * lon_half + jnp.arange(lon_half, dtype=jnp.int32)
        basis = synthesis(all_pairs, lon_block, lon_total)
        pieces.append(
            jnp.einsum(
                "psfhr,rhpj->fsj", spectral, basis, preferred_element_type=jnp.float32
            ).astype(jnp.bfloat16)
        )
    grid = jnp.concatenate(pieces, axis=2)
    fields = grid.reshape(grid_shape[0], 4, grid_shape[1], lon_total)
    level_ids = lax.axis_index("lev") * grid_shape[0] + lax.broadcasted_iota(
        jnp.int32, grid_shape, 0
    )
    row_ids = lax.axis_index("band") * grid_shape[1] + lax.broadcasted_iota(
        jnp.int32, grid_shape, 1
    )
    lon_ids = lax.broadcasted_iota(jnp.int32, grid_shape, 2)
    row_offset = cells[0] - row_ids
    lon_offset = (cells[1] - lon_ids + 2) % lon_total - 2
    level_offset = cells[2] - level_ids
    padded = with_halo(fields, (("band", 2), ("lev", 0)), 2)
    wind_copies = rolled_copies(padded)
    tracer_ids = (2, 3)
    return departure(
        fields,
        wind_copies,
        wind_copies,
        (0, 1),
        tracer_ids,
        eta_shift,
        row_offset,
        lon_offset,
        level_offset,
    )


def solution(mesh):
    return jax.shard_map(
        per_device,
        mesh=mesh,
        in_specs=(
            P(None, "lev", "band", None),
            P("lev", None, "band", None),
            P("band"),
            P("lev", "band", None),
            P(None, "lev", "band", None),
        ),
        out_specs=(P(None, "lev", "band", None), P(None, "lev", "band", None)),
        check_vma=False,
    )
```

profile of v0, /device:TPU:1, one launch (start us, length us, event | category | flops | bytes accessed | tf_op | source)
XLA Modules:
  0.0 234.5 jit_solution(4671835491107172074)
XLA Ops:
  7.2 0.0 all-gather.2.cloned.1.call-start
  7.2 0.7 all-gather.2.cloned.1.call-update
  7.9 1.3 dynamic-slice
  9.8 0.9 dynamic-update-slice
  10.7 27.4 %all-reduce = s32[320]{0:T(512)S(1)} all-reduce(s32[320]{0:T(512)S(1)} %dynamic-update-slice), channel_id=1, replica_groups=mesh['band'=64,'lev'=8] {'band'}, use_global_device_ids=true, to_apply=%add | all-reduce | flops 320 | bytes 2560
  38.2 0.7 broadcast_subtract_fusion.1
  38.8 0.1 iota_compare_fusion
  38.9 0.9 select_bitcast_fusion.1
  39.8 12.6 %all-gather.2.cloned.1.call-done = bf16[8,64,5,641]{3,1,0,2:T(8,128)(2,1)} async-done(((bf16[1,64,5,641]{3,1,0,2:T(8,128)(2,1)}), bf16[8,64,5,641]{3,1,0,2:T(8,128)(2,1)}) %all-gather.2.cloned.1.call-update) | async-done | bytes 3281936 | tf_op jit(solution)/shard_map/all_gather | solution.py:133
  52.4 4.0 %fusion.23 = bf16[64,5,8,8,2,2]{0,3,2,5,4,1:T(8,128)(2,1)S(1)} fusion(bf16[8,64,5,641]{3,1,0,2:T(8,128)(2,1)} %all-gather.2.cloned.1.call-done, bf16[1,2,8,5,641]{4,2,1,0,3:T(8,128)(2,1)S(1)} %get-tuple-element.49, bf16[1,2,8,5,641]{4,2,1,0,3:T(8,128)(2,1)S(1)} %get-tuple-element.48), kind=kOutput, calls=%fused_computation.479 | convolution fusion | flops 105513600 | bytes 3650880 | tf_op jit(solution)/shard_map/scpk,hrfpk->cpsfhr/dot_general | solution.py:124
  56.4 0.3 copy.41
  56.7 1.0 copy.42
  57.7 13.0 %all-to-all-start = ((bf16[64,5,256]{2,1,0:T(8,128)(2,1)}), bf16[64,5,256]{2,1,0:T(8,128)(2,1)S(1)}, u32[]{:S(2)}, u32[]{:S(2)}) async-start(bf16[64,5,256]{2,1,0:T(8,128)(2,1)} %copy.42), calls=%async_computation | async-start | bytes 524288 | tf_op jit(solution)/shard_map/all_to_all | solution.py:135
  70.7 32.7 %multiply_convert_fusion.1 = (bf16[1,2,320,1408]{3,2,0,1:T(8,128)(2,1)}, bf16[1,2,320,1408]{3,2,0,1:T(8,128)(2,1)}, bf16[1,2,320,1408]{3,2,0,1:T(8,128)(2,1)S(1)}, bf16[1,2,320,1408]{3,2,0,1:T(8,128)(2,1)}) fusion(s32[1408]{0:T(1024)S(1)} %iota_add_fusion, s32[2,320]{1,0:T(2,128)S(1)} %pad_add_fusion, f32[2,320]{1,0:T(2,128)S(1)} %get-tuple-element.54, ...), kind=kLoop, calls=%fused_computation.407 | loop fusion | flops 23429120 | bytes 7222272 | tf_op jit(solution)/shard_map/convert.504
  103.5 0.0 all-to-all-done
  103.5 7.4 %copy.43 = bf16[64,5,256]{1,0,2:T(8,128)(2,1)} copy(bf16[64,5,256]{2,1,0:T(8,128)(2,1)S(1)} %all-to-all-done) | data formatting | bytes 327680 | tf_op jit(solution)/shard_map/all_to_all | solution.py:135
  110.9 7.1 %reshape.1137 = bf16[320,8,8,2,2]{0,4,3,2,1:T(2,128)(2,1)S(1)} reshape(bf16[64,5,256]{1,0,2:T(8,128)(2,1)} %copy.43) | data formatting | bytes 327680 | tf_op jit(solution)/shard_map/reshape | solution.py:138
  118.0 0.0 copy-start.1
  118.0 2.8 %fusion.19 = bf16[8,8,1408]{2,0,1:T(8,128)(2,1)S(1)} fusion(bf16[1,2,320,1408]{3,2,0,1:T(8,128)(2,1)} %get-tuple-element.51, bf16[1,2,320,1408]{3,2,0,1:T(8,128)(2,1)} %get-tuple-element.50, bf16[320,8,8,2,2]{0,4,3,2,1:T(2,128)(2,1)S(1)} %reshape.1137), kind=kOutput, calls=%fused_computation.425 | convolution fusion | flops 237985792 | bytes 3948544 | tf_op jit(solution)/shard_map/psfhr,rhpj->fsj/dot_general | solution.py:146
  120.9 0.0 copy-done.1
  120.9 0.7 fusion.18
  121.6 0.1 reshape.1138
  121.7 0.1 constant_dynamic-update-slice_fusion.4
  121.8 0.1 fusion.1461
  121.9 2.9 %collective-permute-start = (bf16[2,4,2,2816]{3,2,0,1:T(2,128)(2,1)S(1)}, bf16[2,4,2,2816]{3,2,0,1:T(2,128)(2,1)S(1)}, u32[]{:S(2)}, u32[]{:S(2)}) collective-permute-start(bf16[2,4,2,2816]{3,2,0,1:T(2,128)(2,1)S(1)} %get-tuple-element.47), channel_id=1, source_target_pairs={{0,8},{8,16},{16,24},{24,32},{32,40},{40,48},{48,56},{56,64},{64,7... | collective-permute-start | bytes 270344 | tf_op jit(solution)/shard_map/ppermute | solution.py:22
  124.8 1.3 collective-permute-start.1
  126.1 0.2 collective-permute-done
  126.4 0.2 copy_dynamic-update-slice_fusion.2
  126.6 3.5 %collective-permute-done.1 = bf16[2,4,2,2816]{3,2,0,1:T(2,128)(2,1)S(1)} collective-permute-done((bf16[2,4,2,2816]{3,2,0,1:T(2,128)(2,1)S(1)}, bf16[2,4,2,2816]{3,2,0,1:T(2,128)(2,1)S(1)}, u32[]{:S(2)}, u32[]{:S(2)}) %collective-permute-start.1) | collective-permute-done | bytes 90144 | tf_op jit(solution)/shard_map/ppermute | solution.py:23
  130.1 0.1 copy_dynamic-update-slice_fusion.3
  130.2 4.2 %collective-permute-start.2 = (bf16[2,4,12,2816]{3,1,2,0:T(4,128)(2,1)S(1)}, bf16[2,4,12,2816]{3,1,2,0:T(4,128)(2,1)S(1)}, u32[]{:S(2)}, u32[]{:S(2)}) collective-permute-start(bf16[2,4,12,2816]{3,1,2,0:T(4,128)(2,1)S(1)} %copy_dynamic-update-slice_fusion.3), channel_id=1, source_target_pairs={{0,1},{1,2},{2,3},{3,4},{4,5},{5,6},{6,7},{8,9},{9,10},{10,11},{11... | collective-permute-start | bytes 1622024 | tf_op jit(solution)/shard_map/ppermute | solution.py:22
  134.4 2.1 collective-permute-start.3
  136.5 0.1 constant_dynamic-update-slice_fusion.3
  136.6 4.0 %collective-permute-done.2 = bf16[2,4,12,2816]{3,1,2,0:T(4,128)(2,1)S(1)} collective-permute-done((bf16[2,4,12,2816]{3,1,2,0:T(4,128)(2,1)S(1)}, bf16[2,4,12,2816]{3,1,2,0:T(4,128)(2,1)S(1)}, u32[]{:S(2)}, u32[]{:S(2)}) %collective-permute-start.2) | collective-permute-done | bytes 540704 | tf_op jit(solution)/shard_map/ppermute | solution.py:22
  140.7 0.2 fusion.1459
  140.9 0.1 copy_dynamic-update-slice_fusion
  141.0 4.1 %collective-permute-done.3 = bf16[2,4,12,2816]{3,1,2,0:T(4,128)(2,1)S(1)} collective-permute-done((bf16[2,4,12,2816]{3,1,2,0:T(4,128)(2,1)S(1)}, bf16[2,4,12,2816]{3,1,2,0:T(4,128)(2,1)S(1)}, u32[]{:S(2)}, u32[]{:S(2)}) %collective-permute-start.3) | collective-permute-done | bytes 540704 | tf_op jit(solution)/shard_map/ppermute | solution.py:23
  145.1 0.1 fusion.1460
  145.2 0.1 fusion.1455
  145.3 1.0 fusion.1456
  146.3 0.1 fusion.1457
  146.4 1.0 fusion.1458
  147.4 0.3 fusion.35
  147.7 0.0 copy-start
  147.7 0.0 copy-start.2
  147.7 2.6 %fusion.44 = (bf16[2,1,8,2816]{3,1,2,0:T(2,128)(2,1)S(1)}, bf16[2,1,8,2816]{3,1,2,0:T(2,128)(2,1)S(1)}, bf16[2,1,8,2816]{3,1,2,0:T(2,128)(2,1)S(1)}, bf16[2,1,8,...) fusion(bf16[2,4,12,2816]{3,1,2,0:T(4,128)(2,1)S(1)} %copy_dynam, ...), kind=kLoop, calls=%fused_computation.1032 | loop fusion | flops 405504 | bytes 1892352 | tf_op jit(solution)/shard_map/concatenate | solution.py:24
  150.3 2.3 fusion.45
  152.6 0.0 copy-done
  152.6 0.0 copy-done.2
  152.6 12.2 %subtract_clamp_fusion.3 = (f32[2,8,2816]{2,1,0:T(8,128)S(1)}, f32[2,8,2816]{2,1,0:T(8,128)S(1)}, pred[2,8,2816]{2,1,0:T(8,128)(4,1)S(1)}, pred[2,8,2816]{2,1,0:T(8,128)(4,1)S(1)}) fusion(s32[3,2,8,2816]{3,2,1,0:T(8,128)S(1)} %copy-done, s32[8]{0:T(128)S(1)} %iota_add_fusion.1, bf16[2,4,12,2816]{3,2,0,1:T(8,128)(2,1)S(1)} %get-tuple-element.37, ...), kind=kLoop, calls=%fused_computation.2252 | loop fusion | flops 42037248 | bytes 13190144 | tf_op jit(solution)/shard_map/jit(clip)/min | solution.py:38
  164.8 11.9 %subtract_clamp_fusion.2 = f32[2,8,2816]{2,1,0:T(8,128)S(1)} fusion(bf16[2,4,12,2816]{3,2,0,1:T(8,128)(2,1)S(1)} %get-tuple-element.37, bf16[4,4,12,2816]{3,2,0,1:T(8,128)(2,1)S(1)} %get-tuple-element.40, bf16[2,4,10,2816]{3,2,0,1:T(8,128)(2,1)S(1)} %constant_dynamic-update-slice_fusion.3, bf16[2,4,12,2816]{3,2,0,1:T(8,128)(2,1)S(1)} %get-tuple-element.42, ...), kind=kLoop, calls=%fused_computation.2250 | loop fusion | flops 41676800 | bytes 12919296 | tf_op jit(solution)/shard_map/jit(clip)/min | solution.py:38
  176.7 37.6 %fusion.1445 = (bf16[1,2,8,2816]{3,2,1,0:T(8,128)(2,1)S(1)}, f32[2,8,2816]{2,1,0:T(8,128)S(1)}, f32[2,8,2816]{2,1,0:T(8,128)S(1)}) fusion(bf16[6,4,12,2]{3,2,0,1:T(8,128)(2,1)S(1)} %get-tuple-element.10, bf16[6,4,12,1]{3,2,0,1:T(8,128)(2,1)S(1)} %get-tuple-element.14, bf16[2,4,12,2816]{3,2,0,1:T(8,128)(2,1)S(1)} %get-tuple-element.42, ...), kind=kLoop, calls=%fused_computation.2801 | loop fusion | flops 117370880 | bytes 18506240 | tf_op jit(solution)/shard_map/stack | solution.py:101
  214.3 11.9 %fusion.1446 = bf16[1,2,8,2816]{3,2,1,0:T(8,128)(2,1)S(1)} fusion(bf16[6,4,12,2]{3,2,0,1:T(8,128)(2,1)S(1)} %get-tuple-element.10, bf16[6,4,12,2814]{3,2,0,1:T(8,128)(2,1)S(1)} %get-tuple-element.12, bf16[6,4,12,1]{3,2,0,1:T(8,128)(2,1)S(1)} %get-tuple-element.14, bf16[6,4,12,2815]{3,2,0,1:T(8,128)(2,1)S(1)} %get-tuple-element.16, ...), kind=kLoop, calls=%fused_computation.2802 | loop fusion | flops 41316352 | bytes 13099520 | tf_op jit(solution)/shard_map/stack | solution.py:101
  226.2 0.7 pad_maximum_fusion.3
  226.9 0.8 pad_maximum_fusion.1
  (11 shorter events, 0.1 us)
Async XLA Ops:
  7.2 45.2 %all-gather.2.cloned.1.call-start = ((), (), s32[]{:S(2)}) async-start(), calls=%async_computation.1 | async-start | bytes 4423680 | tf_op jit(solution)/shard_map/all_gather | solution.py:133
  57.7 45.8 %all-to-all-start = ((bf16[64,5,256]{2,1,0:T(8,128)(2,1)}), bf16[64,5,256]{2,1,0:T(8,128)(2,1)S(1)}, u32[]{:S(2)}, u32[]{:S(2)}) async-start(bf16[64,5,256]{2,1,0:T(8,128)(2,1)} %copy.42), calls=%async_computation | async-start | bytes 524288 | tf_op jit(solution)/shard_map/all_to_all | solution.py:135
  118.0 2.9 %copy-start.1 = (bf16[1,2,320,1408]{3,2,0,1:T(8,128)(2,1)S(1)}, bf16[1,2,320,1408]{3,2,0,1:T(8,128)(2,1)}, u32[]{:S(2)}) copy-start(bf16[1,2,320,1408]{3,2,0,1:T(8,128)(2,1)} %get-tuple-element.53) | copy-start | bytes 5406724
  121.9 4.5 %collective-permute-start = (bf16[2,4,2,2816]{3,2,0,1:T(2,128)(2,1)S(1)}, bf16[2,4,2,2816]{3,2,0,1:T(2,128)(2,1)S(1)}, u32[]{:S(2)}, u32[]{:S(2)}) collective-permute-start(bf16[2,4,2,2816]{3,2,0,1:T(2,128)(2,1)S(1)} %get-tuple-element.47), channel_id=1, source_target_pairs={{0,8},{8,16},{16,24},{24,32},{32,40},{40,48},{48,56},{56,64},{64,7... | collective-permute-start | bytes 270344 | tf_op jit(solution)/shard_map/ppermute | solution.py:22
  124.8 5.3 %collective-permute-start.1 = (bf16[2,4,2,2816]{3,2,0,1:T(2,128)(2,1)S(1)}, bf16[2,4,2,2816]{3,2,0,1:T(2,128)(2,1)S(1)}, u32[]{:S(2)}, u32[]{:S(2)}) collective-permute-start(bf16[2,4,2,2816]{3,2,0,1:T(2,128)(2,1)S(1)} %get-tuple-element.46), channel_id=1, source_target_pairs={{8,0},{16,8},{24,16},{32,24},{40,32},{48,40},{56,48},{64,56},{72,6... | collective-permute-start | bytes 270344 | tf_op jit(solution)/shard_map/ppermute | solution.py:23
  130.2 10.5 %collective-permute-start.2 = (bf16[2,4,12,2816]{3,1,2,0:T(4,128)(2,1)S(1)}, bf16[2,4,12,2816]{3,1,2,0:T(4,128)(2,1)S(1)}, u32[]{:S(2)}, u32[]{:S(2)}) collective-permute-start(bf16[2,4,12,2816]{3,1,2,0:T(4,128)(2,1)S(1)} %copy_dynamic-update-slice_fusion.3), channel_id=1, source_target_pairs={{0,1},{1,2},{2,3},{3,4},{4,5},{5,6},{6,7},{8,9},{9,10},{10,11},{11... | collective-permute-start | bytes 1622024 | tf_op jit(solution)/shard_map/ppermute | solution.py:22
  134.4 10.7 %collective-permute-start.3 = (bf16[2,4,12,2816]{3,1,2,0:T(4,128)(2,1)S(1)}, bf16[2,4,12,2816]{3,1,2,0:T(4,128)(2,1)S(1)}, u32[]{:S(2)}, u32[]{:S(2)}) collective-permute-start(bf16[2,4,12,2816]{3,1,2,0:T(4,128)(2,1)S(1)} %copy_dynamic-update-slice_fusion.3), channel_id=1, source_target_pairs={{1,0},{2,1},{3,2},{4,3},{5,4},{6,5},{7,6},{9,8},{10,9},{11,10},{12... | collective-permute-start | bytes 1622024 | tf_op jit(solution)/shard_map/ppermute | solution.py:23
  147.7 4.9 %copy-start = (s32[3,2,8,2816]{3,2,1,0:T(8,128)S(1)}, s32[3,2,8,2816]{3,2,1,0:T(8,128)}, u32[]{:S(2)}) copy-start(s32[3,2,8,2816]{3,2,1,0:T(8,128)} %param.9) | copy-start | bytes 1622020
  147.7 4.9 %copy-start.2 = (bf16[2,8,2816]{2,1,0:T(8,128)(2,1)S(1)}, bf16[2,8,2816]{2,1,0:T(8,128)(2,1)}, u32[]{:S(2)}) copy-start(bf16[2,8,2816]{2,1,0:T(8,128)(2,1)} %param.8) | copy-start | bytes 270340
Sparse Core Ops, SparseCore 0:
  10.1 42.2 all-gather.1
where the time goes:
time: 236 us; the launch traced here: 235 us
  other arithmetic  115 us (49%)
  blocking collectives  27.4 us (12%)
  waiting for transfers between devices  25.1 us (11%)
  starting transfers between devices  23.6 us (10%)
  local copies, waits for them, and re-layouts  21.3 us (9%)
  between operations  15 us (6%)
  matrix products  7.5 us (3%)
    another operation x3, other arithmetic, departure(): jnp.stack([heat, moisture]).astype(jnp.bfloat16)  50.2 us
    another operation x1, other arithmetic  32.7 us
    unnamed x1, blocking collectives  27.4 us
    min x2, other arithmetic, tap_weights(): fraction = jnp.clip(-shift - offset.astype(jnp.float32), -0.5, 1.5)  24.1 us
    all_to_all x1, starting transfers between devices, per_device(): lax.all_to_all(local_sums, 'band', split_axis=0, concat_axis=1, tiled=True)  13 us
    all_gather x1, waiting for transfers between devices, per_device(): lax.all_gather(legendre, 'lev', axis=0, tiled=True)  12.6 us
    ppermute x2, waiting for transfers between devices, with_halo(): after = lax.ppermute(first, axis, down)  7.62 us
    all_to_all x1, local copies, waits for them, and re-layouts, per_device(): lax.all_to_all(local_sums, 'band', split_axis=0, concat_axis=1, tiled=True)  7.41 us
  transfers between devices with their start and end apart: 6, of which 5 were waited for; matrix products, arithmetic and copies ran while one was open for 16% of the time, Pallas kernels for 0%

commit v1 on v0

v1 whole, which is shorter than its diff:
```python
import functools
import math

import jax
import jax.numpy as jnp
import numpy as np
from jax import lax
from jax.experimental import pallas as pl
from jax.experimental.pallas import tpu as pltpu
from jax.sharding import PartitionSpec as P

ITERS = 2
COURANT = 0.8
MESH = pl.DeviceIdType.MESH
BF16 = jnp.bfloat16
F32 = jnp.float32
TAP = jnp.bfloat16
VMEM_LIMIT = 60 * 1024 * 1024


def nt_dot(a, b):
    return lax.dot_general(a, b, (((1,), (1,)), ((), ())), preferred_element_type=F32)


def tn_dot(a, b):
    return lax.dot_general(a, b, (((0,), (0,)), ((), ())), preferred_element_type=F32)


def comm_kernel(
    nb,
    nx,
    pairs,
    width,
    spec_ref,
    leg_ref,
    pair_ref,
    out_ref,
    specg,
    legs,
    sums_out,
    sums_in,
    stage,
    send,
    recv,
    halo,
    local_sem,
    spec_send,
    spec_recv,
    leg_send,
    leg_recv,
    x_send,
    x_recv,
    band_send,
    band_recv,
    halo_send,
    halo_recv,
):
    b = lax.axis_index("band")
    lev = lax.axis_index("lev")
    nlev = 2 * nx
    x = lev // 2
    core = lev % 2

    load = pltpu.make_async_copy(leg_ref, legs.at[core], local_sem)
    load.start()
    barrier = pltpu.get_barrier_semaphore()

    def greet_band(d, carry):
        pl.semaphore_signal(
            barrier, inc=1, device_id=(lax.rem(b + d, nb), lev), device_id_type=MESH
        )
        return carry

    for d in range(1, nlev):
        pl.semaphore_signal(
            barrier, inc=1, device_id=(b, lax.rem(lev + d, nlev)), device_id_type=MESH
        )
    lax.fori_loop(1, nb, greet_band, 0)
    for p in range(pairs):
        specg[x, p] = jnp.concatenate([spec_ref[0, p], spec_ref[1, p]], axis=0)
    load.wait()
    pl.semaphore_wait(barrier, nb - 1 + nlev - 1)

    spec_copies = []
    for d in range(1, nx):
        copy = pltpu.make_async_remote_copy(
            src_ref=specg.at[x],
            dst_ref=specg.at[x],
            send_sem=spec_send.at[d - 1],
            recv_sem=spec_recv.at[d - 1],
            device_id=(b, 2 * lax.rem(x + d, nx) + core),
            device_id_type=MESH,
        )
        copy.start()
        spec_copies.append(copy)
    leg_copy = pltpu.make_async_remote_copy(
        src_ref=legs.at[core],
        dst_ref=legs.at[core],
        send_sem=leg_send,
        recv_sem=leg_recv,
        device_id=(b, 2 * x + 1 - core),
        device_id_type=MESH,
    )
    leg_copy.start()
    leg_copy.wait()
    for copy in spec_copies:
        copy.wait()

    columns = lax.broadcasted_iota(jnp.int32, (16, width), 1)
    nothing = jnp.zeros((16, width), F32)
    for p in range(pairs):
        first_part = columns < (width - 1 - pair_ref[p])
        parts = []
        for other in range(nx):
            values = specg[other, p].astype(F32)
            parts.append(jnp.where(first_part, values, nothing))
            parts.append(jnp.where(first_part, nothing, values))
        rows = jnp.concatenate(parts, axis=0).astype(BF16)
        table = jnp.concatenate([legs[0, p], legs[1, p]], axis=0)
        total = nt_dot(rows, table).astype(BF16)
        for other in range(nx):
            sums_out[other, p] = total[other * 32 : (other + 1) * 32]
    sums_in[x] = sums_out[x]
    x_copies = []
    for d in range(1, nx):
        partner = lax.rem(x + d, nx)
        copy = pltpu.make_async_remote_copy(
            src_ref=sums_out.at[partner],
            dst_ref=sums_in.at[x],
            send_sem=x_send.at[d - 1],
            recv_sem=x_recv.at[d - 1],
            device_id=(b, 2 * partner + core),
            device_id_type=MESH,
        )
        copy.start()
        x_copies.append(copy)

    lanes = nx * 32
    lane = lax.broadcasted_iota(jnp.int32, (nb, lanes), 1)
    band = lax.broadcasted_iota(jnp.int32, (nb, lanes), 0)
    numbers = jnp.zeros((nb, lanes), jnp.int32)
    for p in range(pairs):
        numbers = jnp.where(lane == 2 * p, pair_ref[p] // 128, numbers)
        numbers = jnp.where(lane == 2 * p + 1, pair_ref[p] % 128, numbers)
    stage[pl.ds(3 * pairs, nb, stride=16), :] = numbers.astype(F32)
    square = (2 * nb, 2 * nb)
    unit = jnp.where(
        lax.broadcasted_iota(jnp.int32, square, 0) == lax.broadcasted_iota(jnp.int32, square, 1),
        1.0,
        0.0,
    ).astype(BF16)
    before = (lane // 32) % 2 == 0
    outside = ((band == 0) & before) | ((band == nb - 1) & jnp.logical_not(before))
    for copy in x_copies:
        copy.wait()
    for p in range(pairs):
        block = jnp.concatenate([sums_in[other, p] for other in range(nx)], axis=0)
        turned = nt_dot(unit, block)
        low, high = turned[:nb], turned[nb:]
        stage[pl.ds(2 * p, nb, stride=16), :] = low
        stage[pl.ds(2 * p + 1, nb, stride=16), :] = high
        edge = jnp.where(lane < 64, pltpu.roll(low, 32, 1), pltpu.roll(high, 96, 1))
        edge = jnp.where(before, pltpu.roll(edge, 1, 0), pltpu.roll(edge, nb - 1, 0))
        edge = jnp.where(outside, 0.0, edge)
        stage[pl.ds(2 * pairs + p, nb, stride=16), :] = edge
    send[...] = stage[...].reshape(nb, 16, lanes).astype(BF16)
    recv[b] = send[b]

    def send_band(d, carry):
        target = lax.rem(b + d, nb)
        pltpu.make_async_remote_copy(
            src_ref=send.at[target],
            dst_ref=recv.at[b],
            send_sem=band_send,
            recv_sem=band_recv,
            device_id=(target, lev),
            device_id_type=MESH,
        ).start()
        return carry

    lax.fori_loop(1, nb, send_band, 0)
    every = pltpu.make_async_remote_copy(
        src_ref=send.at[pl.ds(0, nb - 1)],
        dst_ref=recv.at[pl.ds(0, nb - 1)],
        send_sem=band_send,
        recv_sem=band_recv,
        device_id=(lax.rem(b + 1, nb), lev),
        device_id_type=MESH,
    )
    every.wait_recv()

    above = pltpu.make_async_remote_copy(
        src_ref=recv,
        dst_ref=halo.at[0],
        send_sem=halo_send.at[0],
        recv_sem=halo_recv.at[0],
        device_id=(b, lax.rem(lev + 1, nlev)),
        device_id_type=MESH,
    )
    below = pltpu.make_async_remote_copy(
        src_ref=recv,
        dst_ref=halo.at[1],
        send_sem=halo_send.at[1],
        recv_sem=halo_recv.at[1],
        device_id=(b, lax.rem(lev + nlev - 1, nlev)),
        device_id_type=MESH,
    )

    @pl.when(lev < nlev - 1)
    def _():
        above.start()

    @pl.when(lev > 0)
    def _():
        below.start()

    out_ref[1] = recv[...]
    every.wait_send()

    @pl.when(lev > 0)
    def _():
        above.wait_recv()
        out_ref[0] = halo[0]

    @pl.when(lev == 0)
    def _():
        out_ref[0] = jnp.zeros(halo.shape[1:], BF16)

    @pl.when(lev < nlev - 1)
    def _():
        below.wait_recv()
        out_ref[2] = halo[1]
        above.wait_send()

    @pl.when(lev == nlev - 1)
    def _():
        out_ref[2] = jnp.zeros(halo.shape[1:], BF16)

    @pl.when(lev > 0)
    def _():
        below.wait_send()


def gather_sums(spectra, legendre, pairing, nb, nx):
    pairs, width = spectra.shape[2], spectra.shape[3]
    spec = jnp.transpose(spectra, (0, 2, 1, 3))
    table = jnp.transpose(legendre[0], (1, 0, 2))
    lanes = nx * 32
    dma = pltpu.SemaphoreType.DMA
    return pl.pallas_call(
        functools.partial(comm_kernel, nb, nx, pairs, width),
        out_shape=jax.ShapeDtypeStruct((3, nb, 16, lanes), BF16),
        in_specs=[
            pl.BlockSpec(memory_space=pltpu.VMEM),
            pl.BlockSpec(memory_space=pl.ANY),
            pl.BlockSpec(memory_space=pltpu.SMEM),
        ],
        out_specs=pl.BlockSpec(memory_space=pltpu.VMEM),
        scratch_shapes=[
            pltpu.VMEM((nx, pairs, 16, width), BF16),
            pltpu.VMEM((2, pairs, nb, width), BF16),
            pltpu.VMEM((nx, pairs, 32, 2 * nb), BF16),
            pltpu.VMEM((nx, pairs, 32, 2 * nb), BF16),
            pltpu.VMEM((nb * 16, lanes), F32),
            pltpu.VMEM((nb, 16, lanes), BF16),
            pltpu.VMEM((nb, 16, lanes), BF16),
            pltpu.VMEM((2, nb, 16, lanes), BF16),
            dma,
            dma((nx - 1,)),
            dma((nx - 1,)),
            dma,
            dma,
            dma((nx - 1,)),
            dma((nx - 1,)),
            dma,
            dma,
            dma((2,)),
            dma((2,)),
        ],
        compiler_params=pltpu.CompilerParams(
            collective_id=0, has_side_effects=True, vmem_limit_bytes=VMEM_LIMIT
        ),
        name="sums",
    )(spec, table, pairing)


def lagrange_taps(shift, back):
    here = back == 0.0
    x = jnp.clip(back - shift, -0.5, 1.5)
    xm1, xm2, xp1 = x - 1.0, x - 2.0, x + 1.0
    tail = xm1 * xm2
    head = xp1 * x
    first = x * tail * (-1.0 / 6.0)
    second = xp1 * tail * 0.5
    third = head * xm2 * -0.5
    fourth = head * xm1 * (1.0 / 6.0)
    return (
        jnp.where(here, 0.0, first),
        jnp.where(here, first, second),
        jnp.where(here, second, third),
        jnp.where(here, third, fourth),
        jnp.where(here, fourth, 0.0),
    )


def weighted(taps, values):
    total = taps[0] * values[0]
    for tap, value in zip(taps[1:], values[1:]):
        total = total + tap * value
    return total


def fields_kernel(
    nb,
    nq,
    pairs,
    sums_ref,
    basis_ref,
    eta_ref,
    cells_ref,
    adv_ref,
    disp_ref,
    wide,
    slots,
    place,
    orders,
    coef,
    grid,
    near,
    points,
    eta_wide,
    found,
    adv_wide,
):
    qp = grid.shape[0] // 8 * 8 // 288
    npairs = nb * pairs
    kpad = place.shape[1]
    units = qp // 8
    rows = 8
    row0 = lax.axis_index("band") * rows
    lev0 = lax.axis_index("lev") * 2

    for g in range(3):
        wide[...] = sums_ref[g].astype(F32).reshape(nb * 16, 128)
        for p in range(pairs):
            for t, at in enumerate((2 * p, 2 * p + 1, 2 * pairs + p)):
                slots[p * nb : (p + 1) * nb, (g * 3 + t) * 128 : (g * 3 + t + 1) * 128] = wide[
                    pl.ds(at, nb, stride=16), :
                ].astype(BF16)
        if g == 1:
            numbers = wide[pl.ds(3 * pairs, nb, stride=16), :]
            order = lax.broadcasted_iota(jnp.int32, (nb, kpad), 1).astype(F32)
            for p in range(pairs):
                number = numbers[:, 2 * p : 2 * p + 1] * 128.0 + numbers[:, 2 * p + 1 : 2 * p + 2]
                place[p * nb : (p + 1) * nb, :] = jnp.where(order == number, 1.0, 0.0).astype(BF16)
    orders[...] = tn_dot(slots[...], place[...]).reshape(144, 8, kpad)
    for part in range(4):
        coef[:, part * kpad : (part + 1) * kpad] = jnp.concatenate(
            [orders[4 * m + part] for m in range(36)], axis=0
        ).astype(BF16)

    def synthesise(n, carry):
        values = jnp.dot(coef[...], basis_ref[n], preferred_element_type=F32).astype(BF16).astype(F32)
        width = values.shape[1] // 128
        for m in range(36):
            g, t, xs = m // 12, (m // 4) % 3, m % 4
            row = 2 + 2 * xs + t if t < 2 else (xs // 2 + (xs % 2) * 10)
            base = (row * 3 + g) * 8 * qp + 1
            for w in range(width):
                grid[pl.ds(base + n * width + w, 8, stride=qp), :] = values[
                    m * 8 : (m + 1) * 8, w * 128 : (w + 1) * 128
                ]
        return carry

    lax.fori_loop(0, basis_ref.shape[0], synthesise, 0)
    grid[pl.ds(0, 288, stride=qp), :] = grid[pl.ds(nq, 288, stride=qp), :]
    grid[pl.ds(nq + 1, 288, stride=qp), :] = grid[pl.ds(1, 288, stride=qp), :]

    lane = lax.broadcasted_iota(jnp.int32, (qp, 128), 1)

    def shift_rows(n, carry):
        row, field = n // 4, n % 4
        for step in range(5):
            c = step - 2
            moved = []
            for level in range(6):
                base = ((row * 6 + level) * 4 + field) * qp
                here = grid[pl.ds(base + 1, qp), :]
                if c > 0:
                    after = grid[pl.ds(base + 2, qp), :]
                    here = pltpu.roll(jnp.where(lane >= c, here, after), 128 - c, 1)
                elif c < 0:
                    ahead = grid[pl.ds(base, qp), :]
                    here = pltpu.roll(jnp.where(lane < 128 + c, here, ahead), -c, 1)
                moved.append(here)
            for a in range(5):
                pair = jnp.concatenate([moved[a], moved[a + 1]], axis=0).astype(TAP)
                for u in range(units):
                    near[row, u, field, step, a] = pair[u * 16 : (u + 1) * 16]
        return carry

    lax.fori_loop(0, 48, shift_rows, 0)

    for k in range(2):
        eta_wide[...] = eta_ref[k].astype(F32).reshape(nq * 8, 128)
        lon = (
            lax.broadcasted_iota(jnp.int32, (nq, 128), 0) * 128
            + lax.broadcasted_iota(jnp.int32, (nq, 128), 1)
        )
        for i in range(rows):
            part = pl.ds(i, nq, stride=8)
            at = pl.ds(k * qp, nq)
            points[i, 0, at, :] = jnp.where(cells_ref[0, k, part, :] == row0 + i, 0.0, 1.0)
            points[i, 1, at, :] = jnp.where(cells_ref[1, k, part, :] == lon, 0.0, 1.0)
            points[i, 2, at, :] = jnp.where(cells_ref[2, k, part, :] == lev0 + k, 0.0, 1.0)
            points[i, 3, at, :] = eta_wide[part, :]

    def depart(n, carry):
        i, u = n // units, n % units
        at = pl.ds(pl.multiple_of(u * 16, 16), 16)
        row_back, lon_back = points[i, 0, at, :], points[i, 1, at, :]
        level_taps = [
            tap.astype(TAP) for tap in lagrange_taps(points[i, 3, at, :], points[i, 2, at, :])
        ]

        def level_sums(field):
            return [
                [
                    weighted(level_taps, [near[i + b, u, field, c, a] for a in range(5)])
                    for c in range(5)
                ]
                for b in range(5)
            ]

        def horizontal(sums, row_taps, lon_taps):
            return weighted(row_taps, [weighted(lon_taps, sums[b]).astype(F32) for b in range(5)])

        east = near[i + 2, u, 0, 2, 2].astype(F32)
        north = near[i + 2, u, 1, 2, 2].astype(F32)
        east_sums, north_sums = level_sums(0), level_sums(1)
        shift_row, shift_lon = COURANT * north, COURANT * east
        for sweep in range(ITERS):
            row_taps = lagrange_taps(shift_row, row_back)
            lon_taps = [tap.astype(TAP) for tap in lagrange_taps(shift_lon, lon_back)]
            shift_row = 0.5 * COURANT * (north + horizontal(north_sums, row_taps, lon_taps))
            shift_lon = 0.5 * COURANT * (east + horizontal(east_sums, row_taps, lon_taps))
        found[i, 0, at, :] = shift_row
        found[i, 1, at, :] = shift_lon
        row_taps = lagrange_taps(shift_row, row_back)
        lon_taps = [tap.astype(TAP) for tap in lagrange_taps(shift_lon, lon_back)]
        found[i, 2, at, :] = horizontal(level_sums(2), row_taps, lon_taps)
        found[i, 3, at, :] = horizontal(level_sums(3), row_taps, lon_taps)
        return carry

    lax.fori_loop(0, rows * units, depart, 0)
    for k in range(2):
        for i in range(rows):
            part = pl.ds(i, nq, stride=8)
            at = pl.ds(k * qp, nq)
            for which in range(2):
                disp_ref[which, k, part, :] = found[i, which, at, :]
                adv_wide[which, k, part, :] = found[i, 2 + which, at, :]
    adv_ref[...] = adv_wide[...].reshape(adv_ref.shape).astype(BF16)


def basis_table(total, lon_total, block):
    npairs = total // 2
    kpad = -(-npairs // 128) * 128
    r = np.arange(npairs, dtype=np.int64)
    j = np.arange(lon_total, dtype=np.int64)
    table = np.zeros((2, 2, kpad, lon_total), np.float32)
    for half, order in enumerate((r, total - 1 - r)):
        angle = (2.0 * math.pi / lon_total) * ((order[:, None] * j[None, :]) % lon_total)
        weight = np.where(order == 0, 1.0, 2.0)[:, None]
        table[half, 0, :npairs] = weight * np.cos(angle)
        table[half, 1, :npairs] = -weight * np.sin(angle)
    table = table.reshape(4 * kpad, lon_total // block, block).transpose(1, 0, 2)
    return jnp.asarray(table.astype(BF16)), kpad


def depart_fields(sums, eta_shift, cells, nb, pairs, total):
    lon_total = eta_shift.shape[2]
    nq = lon_total // 128
    qp = -(-(nq + 2) // 8) * 8
    basis, kpad = basis_table(total, lon_total, 256)
    tiles = lambda a: jnp.swapaxes(a.reshape(a.shape[:-1] + (nq, 128)), -3, -2)
    eta = tiles(eta_shift)
    cells = tiles(cells).reshape(3, 2, nq * 8, 128)
    vmem = pl.BlockSpec(memory_space=pltpu.VMEM)
    adv, disp = pl.pallas_call(
        functools.partial(fields_kernel, nb, nq, pairs),
        out_shape=(
            jax.ShapeDtypeStruct((2, 2, nq, 8, 128), BF16),
            jax.ShapeDtypeStruct((2, 2, nq * 8, 128), F32),
        ),
        in_specs=[vmem] * 4,
        out_specs=(vmem, vmem),
        scratch_shapes=[
            pltpu.VMEM((nb * 16, 128), F32),
            pltpu.VMEM((nb * pairs, 9 * 128), BF16),
            pltpu.VMEM((nb * pairs, kpad), BF16),
            pltpu.VMEM((144, 8, kpad), F32),
            pltpu.VMEM((288, 4 * kpad), BF16),
            pltpu.VMEM((288 * qp + 8, 128), F32),
            pltpu.VMEM((12, qp // 8, 4, 5, 5, 16, 128), TAP),
            pltpu.VMEM((8, 4, 2 * qp, 128), F32),
            pltpu.VMEM((nq * 8, 128), F32),
            pltpu.VMEM((8, 4, 2 * qp, 128), F32),
            pltpu.VMEM((2, 2, nq * 8, 128), F32),
        ],
        compiler_params=pltpu.CompilerParams(vmem_limit_bytes=VMEM_LIMIT),
        name="fields",
    )(sums, basis, eta, cells)
    whole = lambda a: jnp.swapaxes(a, -3, -2).reshape(2, 2, 8, lon_total)
    return whole(adv), whole(disp.reshape(2, 2, nq, 8, 128))


def per_device(spectra, legendre, pairing, eta_shift, cells):
    nb = legendre.shape[1]
    pairs, width = spectra.shape[2], spectra.shape[3]
    nx = lax.axis_size("lev") // 2
    sums = gather_sums(spectra, legendre, pairing, nb, nx)
    return depart_fields(sums, eta_shift, cells, nb, pairs, width - 1)


def solution(mesh):
    return jax.shard_map(
        per_device,
        mesh=mesh,
        in_specs=(
            P(None, "lev", "band", None),
            P("lev", None, "band", None),
            P("band"),
            P("lev", "band", None),
            P(None, "lev", "band", None),
        ),
        out_specs=(P(None, "lev", "band", None), P(None, "lev", "band", None)),
        check_vma=False,
    )
```

time: 236 us -> 67.2 us (0.28)
  other arithmetic: 115 us -> 0 us
  Pallas kernels: 0 us -> 66.4 us
  blocking collectives: 27.4 us -> 0 us
  waiting for transfers between devices: 25.1 us -> 0 us
  starting transfers between devices: 23.6 us -> 0 us
  local copies, waits for them, and re-layouts: 21.3 us -> 0 us
  between operations: 15 us -> 0.64 us
  matrix products: 7.5 us -> 0 us
    another operation x7 -> x0, other arithmetic: 84.7 us -> none  [the longest x3 50.2 us: departure(): jnp.stack([heat, moisture]).astype(jnp.bfloat16)]
    pallas_call x0 -> x2, Pallas kernels: none -> 66.4 us  [the longest x1 44.3 us: gather_sums(): pl.pallas_call(functools.partial(comm_kernel, nb, nx, pairs, width), out_...]
    unnamed x1 -> x0, blocking collectives: 27.4 us -> none
    min x2 -> x0, other arithmetic: 24.1 us -> none  [tap_weights(): fraction = jnp.clip(-shift - offset.astype(jnp.float32), -0.5, 1.5)]
    all_to_all x1 -> x0, starting transfers between devices: 13 us -> none  [per_device(): lax.all_to_all(local_sums, 'band', split_axis=0, concat_axis=1, tiled=True)]
    all_gather x1 -> x0, waiting for transfers between devices: 12.6 us -> none  [per_device(): lax.all_gather(legendre, 'lev', axis=0, tiled=True)]
    ppermute x4 -> x0, waiting for transfers between devices: 11.9 us -> none  [the longest x2 7.62 us: with_halo(): after = lax.ppermute(first, axis, down)]
    ppermute x4 -> x0, starting transfers between devices: 10.5 us -> none  [the longest x2 7.12 us: with_halo(): before = lax.ppermute(last, axis, up)]
  transfers between devices with their start and end apart: 6 -> 0, of which waited for: 5 -> 0; matrix products, arithmetic and copies ran while one was open for 16% -> 0% of each run, Pallas kernels for 0% -> 0%
where the time goes in v1:
time: 67.2 us; the launch traced here: 67 us
  Pallas kernels  66.4 us (99%)
    pallas_call x1, Pallas kernels, gather_sums(): pl.pallas_call(functools.partial(comm_kernel, nb, nx, pairs, width), out_...  44.3 us
    pallas_call x1, Pallas kernels, depart_fields(): pl.pallas_call(functools.partial(fields_kernel, nb, nq, pairs), out_shape...  22.1 us

profile of v1, /device:TPU:1, one launch (start us, length us, event | category | flops | bytes accessed | tf_op | source)
XLA Modules:
  0.0 67.0 jit_solution(10553800488934306630)
XLA Ops:
  0.6 44.3 %sums.1.sums_ref = bf16[3,64,16,128]{3,2,1,0:T(8,128)(2,1)} custom-call(bf16[2,5,8,641]{3,2,1,0:T(8,128)(2,1)} %bitcast.22, bf16[5,64,641]{2,1,0:T(8,128)(2,1)} %bitcast.21, s32[5]{0:T(128)} %pair_ref.1), custom_call_target="tpu_custom_call" | custom-call | tf_op jit(solution)/shard_map/sums/pallas_call | solution.py:250
  45.0 22.1 %fields.1 = (bf16[2,2,22,8,128]{4,3,2,1,0:T(8,128)(2,1)}, f32[2,2,176,128]{3,2,1,0:T(8,128)}) custom-call(bf16[3,64,16,128]{3,2,1,0:T(8,128)(2,1)} %sums.1.sums_ref, bf16[11,1536,256]{2,1,0:T(8,128)(2,1)} %constant.2.clone.basis_ref, bf16[2,22,8,128]{3,2,1,0:T(8,128)(2,1)} %bitcast.23, s32[3,2,176,128]{3,2,1,0:T(8,128)} %bitcast.20), custom_call_target="tpu_custom_call" | custom-call | tf_op jit(solution)/shard_map/fields/pallas_call | solution.py:490

commit v2 on v1

v2 whole, which is shorter than its diff:
```python
import functools
import math

import jax
import jax.numpy as jnp
import numpy as np
from jax import lax
from jax.experimental import pallas as pl
from jax.experimental.pallas import tpu as pltpu
from jax.sharding import PartitionSpec as P

ITERS = 2
COURANT = 0.8
MESH = pl.DeviceIdType.MESH
BF16 = jnp.bfloat16
F32 = jnp.float32
TAP = jnp.bfloat16
VMEM_LIMIT = 60 * 1024 * 1024
GROUPS = 8


def nt_dot(a, b):
    return lax.dot_general(a, b, (((1,), (1,)), ((), ())), preferred_element_type=F32)


def tn_dot(a, b):
    return lax.dot_general(a, b, (((0,), (0,)), ((), ())), preferred_element_type=F32)


def comm_kernel(
    nb,
    nx,
    pairs,
    width,
    spec_ref,
    leg_ref,
    pair_ref,
    out_ref,
    raw,
    specg,
    last,
    legs,
    sums_out,
    sums_in,
    stage,
    send,
    recv,
    nothing,
    load_sem,
    last_send,
    last_recv,
    spec_send,
    spec_recv,
    leg_send,
    leg_recv,
    x_send,
    x_recv,
    band_send,
    band_recv,
    halo_send,
    halo_recv,
    own_sem,
    lev_ready,
    band_ready,
):
    b = lax.axis_index("band")
    lev = lax.axis_index("lev")
    nlev = 2 * nx
    x = lev // 2
    core = lev % 2
    group = max(1, nb // GROUPS)

    def remote(src, dst, send_sem, recv_sem, band, level):
        return pltpu.make_async_remote_copy(
            src_ref=src,
            dst_ref=dst,
            send_sem=send_sem,
            recv_sem=recv_sem,
            device_id=(band, level),
            device_id_type=MESH,
        )

    def signal(semaphore, band, level):
        pl.semaphore_signal(semaphore, inc=1, device_id=(band, level), device_id_type=MESH)

    side = math.isqrt(nb)

    def hops(d):
        return sum(min(n, side - n) for n in (d // side, d % side))

    order = sorted(range(1, nb), key=lambda d: -hops(d))
    sibling = (b, 2 * x + 1 - core)

    loads = (
        pltpu.make_async_copy(spec_ref, raw, load_sem.at[0]),
        pltpu.make_async_copy(leg_ref, legs.at[:, core], load_sem.at[1]),
    )
    for load in loads:
        load.start()
    barrier = pltpu.get_barrier_semaphore()

    for d in range(1, nx):
        signal(barrier, b, 2 * lax.rem(x + d, nx))

    @pl.when(core == 1)
    def _():
        signal(barrier, b, 2 * x)

    loads[0].wait()
    tail = jnp.zeros((16, 128), F32)
    place = lax.broadcasted_iota(jnp.int32, (16, 128), 1)
    for p in range(pairs):
        own = jnp.concatenate([raw[0, p], raw[1, p]], axis=0)
        specg[p, 0] = own[:, : width - 1]
        tail = jnp.where(place == p, own[:, width - 1 :].astype(F32), tail)
    last[0] = tail.astype(BF16)

    @pl.when(core == 0)
    def _():
        pl.semaphore_wait(barrier, nlev - 1)
        signal(lev_ready, *sibling)

    @pl.when(core == 1)
    def _():
        pl.semaphore_wait(lev_ready, 1)

    for p in range(pairs):
        for d in sorted(range(1, nx), key=lambda d: -min(d, nx - d)):
            target = 2 * lax.rem(x + d, nx) + core
            if p == 0:
                remote(last.at[0], last.at[d], last_send, last_recv, b, target).start()
            remote(specg.at[p, 0], specg.at[p, d], spec_send, spec_recv.at[p], b, target).start()
        if p == 0:
            loads[1].wait()
        remote(legs.at[p, core], legs.at[p, core], leg_send, leg_recv.at[p], *sibling).start()

    for d in order:
        signal(barrier, lax.rem(b + d, nb), 2 * x + 1)
    nothing[...] = jnp.zeros(nothing.shape, BF16)

    columns = lax.broadcasted_iota(jnp.int32, (16, width - 1), 1)
    zero = jnp.zeros((16, width - 1), F32)
    no_tail = jnp.zeros((16, 1), F32)
    others = last.at[pl.ds(1, nx - 1)]
    remote(others, others, last_send, last_recv, *sibling).wait_recv()
    for p in range(pairs):
        others = specg.at[p, pl.ds(1, nx - 1)]
        remote(others, others, spec_send, spec_recv.at[p], *sibling).wait_recv()
        table_ref = legs.at[p, 0]
        remote(table_ref, table_ref, leg_send, leg_recv.at[p], *sibling).wait_recv()
        first_part = columns < (width - 1 - pair_ref[p])
        parts = []
        for d in range(nx):
            values = specg[p, d].astype(F32)
            tail = last[d].astype(F32)[:, p : p + 1]
            parts.append(jnp.concatenate([jnp.where(first_part, values, zero), no_tail], axis=1))
            parts.append(jnp.concatenate([jnp.where(first_part, zero, values), tail], axis=1))
        rows = jnp.concatenate(parts, axis=0).astype(BF16)
        table = jnp.concatenate([legs[p, 0], legs[p, 1]], axis=0)
        total = nt_dot(rows, table).astype(BF16)
        for d in range(nx):
            sums_out[p, d] = total[d * 32 : (d + 1) * 32]
        sums_in[p, x] = total[:32]
        for d in range(nx - 1, 0, -1):
            remote(
                sums_out.at[p, d],
                sums_in.at[p, x],
                x_send,
                x_recv.at[p],
                b,
                2 * lax.rem(x + nx - d, nx) + core,
            ).start()

    lanes = nx * 32
    lane = lax.broadcasted_iota(jnp.int32, (nb, lanes), 1)
    band = lax.broadcasted_iota(jnp.int32, (nb, lanes), 0)
    numbers = jnp.zeros((nb, lanes), jnp.int32)
    for p in range(pairs):
        numbers = jnp.where(lane == 2 * p, pair_ref[p] // 128, numbers)
        numbers = jnp.where(lane == 2 * p + 1, pair_ref[p] % 128, numbers)
    stage[pl.ds(3 * pairs, nb, stride=16), :] = numbers.astype(F32)
    square = (2 * nb, 2 * nb)
    unit = jnp.where(
        lax.broadcasted_iota(jnp.int32, square, 0) == lax.broadcasted_iota(jnp.int32, square, 1),
        1.0,
        0.0,
    ).astype(BF16)
    before = (lane // 32) % 2 == 0
    outside = ((band == 0) & before) | ((band == nb - 1) & jnp.logical_not(before))
    for p in range(pairs):
        others = sums_out.at[p, pl.ds(1, nx - 1)]
        remote(others, others, x_send, x_recv.at[p], *sibling).wait_recv()
        block = jnp.concatenate([sums_in[p, other] for other in range(nx)], axis=0)
        turned = nt_dot(unit, block)
        low, high = turned[:nb], turned[nb:]
        stage[pl.ds(2 * p, nb, stride=16), :] = low
        stage[pl.ds(2 * p + 1, nb, stride=16), :] = high
        edge = jnp.where(lane < 64, pltpu.roll(low, 32, 1), pltpu.roll(high, 96, 1))
        edge = jnp.where(before, pltpu.roll(edge, 1, 0), pltpu.roll(edge, nb - 1, 0))
        edge = jnp.where(outside, 0.0, edge)
        stage[pl.ds(2 * pairs + p, nb, stride=16), :] = edge
    send[...] = stage[...].reshape(nb, 16, lanes).astype(BF16)
    recv[nb - 1] = send[b]

    @pl.when(core == 1)
    def _():
        pl.semaphore_wait(barrier, 2 * (nb - 1))
        signal(band_ready, *sibling)

    @pl.when(core == 0)
    def _():
        pl.semaphore_wait(band_ready, 1)

    for n, d in enumerate(order):
        target = lax.rem(b + d, nb)
        remote(
            send.at[target], recv.at[n], band_send, band_recv.at[n // group], target, lev
        ).start()

    above = (b, lax.rem(lev + 1, nlev))
    below = (b, lax.rem(lev + nlev - 1, nlev))
    lowest = lev == 0
    highest = lev == nlev - 1

    @pl.when(lowest)
    def _():
        pltpu.make_async_copy(nothing, out_ref.at[0], own_sem.at[0]).start()

    @pl.when(highest)
    def _():
        pltpu.make_async_copy(nothing, out_ref.at[2], own_sem.at[0]).start()

    for g in reversed(range(GROUPS)):
        end = min(nb - 1, (g + 1) * group)
        if end > g * group:
            arrived = recv.at[pl.ds(g * group, end - g * group)]
            remote(arrived, arrived, band_send, band_recv.at[g], *sibling).wait_recv()
        part = pl.ds(g * group, group)

        @pl.when(lev < nlev - 1)
        def _():
            remote(
                recv.at[part], out_ref.at[0, part], halo_send.at[0], halo_recv.at[0], *above
            ).start()

        @pl.when(lev > 0)
        def _():
            remote(
                recv.at[part], out_ref.at[2, part], halo_send.at[1], halo_recv.at[1], *below
            ).start()

    own = pltpu.make_async_copy(recv, out_ref.at[1], own_sem.at[1])
    own.start()

    others = last.at[pl.ds(1, nx - 1)]
    remote(others, others, last_send, last_recv, *sibling).wait_send()
    others = specg.at[:, pl.ds(1, nx - 1)]
    remote(others, others, spec_send, spec_recv.at[0], *sibling).wait_send()
    tables = legs.at[:, 0]
    remote(tables, tables, leg_send, leg_recv.at[0], *sibling).wait_send()
    others = sums_out.at[:, pl.ds(1, nx - 1)]
    remote(others, others, x_send, x_recv.at[0], *sibling).wait_send()
    arrived = recv.at[pl.ds(0, nb - 1)]
    remote(arrived, arrived, band_send, band_recv.at[0], *sibling).wait_send()
    own.wait()

    up = remote(recv, out_ref.at[0], halo_send.at[0], halo_recv.at[0], *above)
    down = remote(recv, out_ref.at[2], halo_send.at[1], halo_recv.at[1], *below)

    @pl.when(lev > 0)
    def _():
        up.wait_recv()
        down.wait_send()

    @pl.when(lev < nlev - 1)
    def _():
        down.wait_recv()
        up.wait_send()

    @pl.when(lowest)
    def _():
        pltpu.make_async_copy(nothing, out_ref.at[0], own_sem.at[0]).wait()

    @pl.when(highest)
    def _():
        pltpu.make_async_copy(nothing, out_ref.at[2], own_sem.at[0]).wait()


def gather_sums(spectra, legendre, pairing, nb, nx):
    pairs, width = spectra.shape[2], spectra.shape[3]
    spec = jnp.transpose(spectra, (0, 2, 1, 3))
    table = jnp.transpose(legendre[0], (1, 0, 2))
    lanes = nx * 32
    dma = pltpu.SemaphoreType.DMA
    anywhere = pl.BlockSpec(memory_space=pl.ANY)
    return pl.pallas_call(
        functools.partial(comm_kernel, nb, nx, pairs, width),
        out_shape=jax.ShapeDtypeStruct((3, nb, 16, lanes), BF16),
        in_specs=[anywhere, anywhere, pl.BlockSpec(memory_space=pltpu.SMEM)],
        out_specs=anywhere,
        scratch_shapes=[
            pltpu.VMEM(spec.shape, BF16),
            pltpu.VMEM((pairs, nx, 16, width - 1), BF16),
            pltpu.VMEM((nx, 16, 128), BF16),
            pltpu.VMEM((pairs, 2, nb, width), BF16),
            pltpu.VMEM((pairs, nx, 32, 2 * nb), BF16),
            pltpu.VMEM((pairs, nx, 32, 2 * nb), BF16),
            pltpu.VMEM((nb * 16, lanes), F32),
            pltpu.VMEM((nb, 16, lanes), BF16),
            pltpu.VMEM((nb, 16, lanes), BF16),
            pltpu.VMEM((nb, 16, lanes), BF16),
            dma((2,)),
            dma,
            dma,
            dma,
            dma((pairs,)),
            dma,
            dma((pairs,)),
            dma,
            dma((pairs,)),
            dma,
            dma((GROUPS,)),
            dma((2,)),
            dma((2,)),
            dma((2,)),
            pltpu.SemaphoreType.REGULAR,
            pltpu.SemaphoreType.REGULAR,
        ],
        compiler_params=pltpu.CompilerParams(
            collective_id=0, has_side_effects=True, vmem_limit_bytes=VMEM_LIMIT
        ),
        name="sums",
    )(spec, table, pairing)


def lagrange_taps(shift, back):
    here = back == 0.0
    x = jnp.clip(back - shift, -0.5, 1.5)
    xm1, xm2, xp1 = x - 1.0, x - 2.0, x + 1.0
    tail = xm1 * xm2
    head = xp1 * x
    first = x * tail * (-1.0 / 6.0)
    second = xp1 * tail * 0.5
    third = head * xm2 * -0.5
    fourth = head * xm1 * (1.0 / 6.0)
    return (
        jnp.where(here, 0.0, first),
        jnp.where(here, first, second),
        jnp.where(here, second, third),
        jnp.where(here, third, fourth),
        jnp.where(here, fourth, 0.0),
    )


def weighted(taps, values):
    total = taps[0] * values[0]
    for tap, value in zip(taps[1:], values[1:]):
        total = total + tap * value
    return total


def fields_kernel(
    nb,
    nq,
    pairs,
    sums_hbm,
    basis_ref,
    eta_ref,
    cells_ref,
    adv_ref,
    disp_ref,
    wide,
    slots,
    place,
    orders,
    coef,
    basis,
    grid,
    near,
    eta,
    cells,
    points,
    eta_wide,
    found,
    adv_wide,
    sums_ref,
    basis_sem,
    point_sem,
    sums_sem,
):
    qp = grid.shape[0] // 8 * 8 // 288
    half = nb * pairs // 2
    window = place.shape[1] // 2
    lon_half = nq * 64
    units = qp // 8
    rows = 8
    row0 = lax.axis_index("band") * rows
    lev0 = lax.axis_index("lev") * 2

    sums_copies = [
        pltpu.make_async_copy(sums_hbm.at[g], sums_ref.at[g], sums_sem.at[g]) for g in range(3)
    ]
    for copy in sums_copies:
        copy.start()
    blocks = [(start, min(256, lon_half - start)) for start in range(0, lon_half, 256)]
    basis_copies = []
    for n, (start, size) in enumerate(blocks):
        part = pl.ds(start, size)
        copy = pltpu.make_async_copy(
            basis_ref.at[:, :, part], basis.at[:, :, part], basis_sem.at[n]
        )
        copy.start()
        basis_copies.append(copy)
    point_copies = (
        pltpu.make_async_copy(eta_ref, eta, point_sem.at[0]),
        pltpu.make_async_copy(cells_ref, cells, point_sem.at[1]),
    )
    for copy in point_copies:
        copy.start()

    for g in range(3):
        sums_copies[g].wait()
        wide[...] = sums_ref[g].astype(F32).reshape(nb * 16, 128)
        for p in range(pairs):
            for t, at in enumerate((2 * p, 2 * p + 1, 2 * pairs + p)):
                slots[p * nb : (p + 1) * nb, (g * 3 + t) * 128 : (g * 3 + t + 1) * 128] = wide[
                    pl.ds(at, nb, stride=16), :
                ].astype(BF16)
        if g == 1:
            numbers = wide[pl.ds(3 * pairs, nb, stride=16), :].astype(jnp.int32)
            column = lax.broadcasted_iota(jnp.int32, (nb, 2 * window), 1)
            order = jnp.where(column < window, 2 * column, 2 * (column - window) + 1)
            for p in range(pairs):
                number = numbers[:, 2 * p : 2 * p + 1] * 128 + numbers[:, 2 * p + 1 : 2 * p + 2]
                place[p * nb : (p + 1) * nb, :] = jnp.where(order == number, 1.0, 0.0).astype(BF16)
    orders[...] = tn_dot(slots[...], place[...]).reshape(144, 8, 2 * window)
    for parity in range(2):
        for part in range(4):
            first = window * ((part // 2 + parity) % 2)
            coef[parity, part] = jnp.concatenate(
                [orders[4 * m + part, :, first : first + window] for m in range(36)], axis=0
            ).astype(BF16)

    for (start, size), copy in zip(blocks, basis_copies):
        copy.wait()
        even, odd = [
            sum(
                jnp.dot(
                    coef[parity, part, :, :half],
                    basis[parity, part * half : (part + 1) * half, start : start + size],
                    preferred_element_type=F32,
                )
                for part in range(4)
            )
            for parity in range(2)
        ]
        for turn, values in enumerate((even + odd, even - odd)):
            for m in range(36):
                g, t, xs = m // 12, (m // 4) % 3, m % 4
                row = 2 + 2 * xs + t if t < 2 else (xs // 2 + (xs % 2) * 10)
                base = (row * 3 + g) * 8 * qp + 1 + (start + turn * lon_half) // 128
                for w in range(size // 128):
                    grid[pl.ds(base + w, 8, stride=qp), :] = values[
                        m * 8 : (m + 1) * 8, w * 128 : (w + 1) * 128
                    ]
    grid[pl.ds(0, 288, stride=qp), :] = grid[pl.ds(nq, 288, stride=qp), :]
    grid[pl.ds(nq + 1, 288, stride=qp), :] = grid[pl.ds(1, 288, stride=qp), :]

    lane = lax.broadcasted_iota(jnp.int32, (16, 128), 1).astype(F32).astype(TAP)
    inside = {c: (lane >= c if c > 0 else lane < 128 + c) for c in (-2, -1, 1, 2)}

    def shift_fields(n, carry):
        row, level = n // 6, n % 6
        for two in range(2):
            for t in range(units):

                def block(offset):
                    return jnp.concatenate(
                        [
                            grid[pl.ds((n * 4 + field) * qp + 8 * t + offset, 8), :]
                            for field in (2 * two, 2 * two + 1)
                        ],
                        axis=0,
                    ).astype(TAP)

                ahead, here, after = block(0), block(1), block(2)
                for c in range(-2, 3):
                    value = here
                    if c > 0:
                        value = pltpu.roll(jnp.where(inside[c], here, after), 128 - c, 1)
                    elif c < 0:
                        value = pltpu.roll(jnp.where(inside[c], here, ahead), -c, 1)
                    near[row, level, t, two, c + 2] = value
        return carry

    lax.fori_loop(0, 72, shift_fields, 0, unroll=8)

    for copy in point_copies:
        copy.wait()
    for k in range(2):
        eta_wide[...] = eta[k].astype(F32).reshape(nq * 8, 128)
        lon = (
            lax.broadcasted_iota(jnp.int32, (nq, 128), 0) * 128
            + lax.broadcasted_iota(jnp.int32, (nq, 128), 1)
        )
        for i in range(rows):
            part = pl.ds(i, nq, stride=8)
            at = pl.ds(k * qp, nq)
            points[i, 0, at, :] = jnp.where(cells[0, k, part, :] == row0 + i, 0.0, 1.0)
            points[i, 1, at, :] = jnp.where(cells[1, k, part, :] == lon, 0.0, 1.0)
            points[i, 2, at, :] = jnp.where(cells[2, k, part, :] == lev0 + k, 0.0, 1.0)
            points[i, 3, at, :] = eta_wide[part, :]

    def double(taps):
        return [jnp.concatenate([tap, tap], axis=0).astype(TAP) for tap in taps]

    def depart(n, carry):
        i, k, t = n // (2 * units), (n // units) % 2, n % units
        at = pl.ds(pl.multiple_of((k * units + t) * 8, 8), 8)
        row_back, lon_back = points[i, 0, at, :], points[i, 1, at, :]
        level_taps = double(lagrange_taps(points[i, 3, at, :], points[i, 2, at, :]))

        def level_sums(two):
            return [
                [
                    weighted(level_taps, [near[i + b, k + a, t, two, c] for a in range(5)])
                    for c in range(5)
                ]
                for b in range(5)
            ]

        def horizontal(sums, shift_row, shift_lon):
            row_taps = lagrange_taps(shift_row, row_back)
            lon_taps = double(lagrange_taps(shift_lon, lon_back))
            lines = [weighted(lon_taps, sums[b]).astype(F32) for b in range(5)]
            return [
                weighted(row_taps, [line[s * 8 : (s + 1) * 8] for line in lines]) for s in range(2)
            ]

        wind = near[i + 2, k + 2, t, 0, 2].astype(F32)
        east, north = wind[:8], wind[8:]
        wind_sums = level_sums(0)
        shift_row, shift_lon = COURANT * north, COURANT * east
        for sweep in range(ITERS):
            east_found, north_found = horizontal(wind_sums, shift_row, shift_lon)
            shift_row = 0.5 * COURANT * (north + north_found)
            shift_lon = 0.5 * COURANT * (east + east_found)
        found[i, 0, at, :] = shift_row
        found[i, 1, at, :] = shift_lon
        heat, moisture = horizontal(level_sums(1), shift_row, shift_lon)
        found[i, 2, at, :] = heat
        found[i, 3, at, :] = moisture
        return carry

    lax.fori_loop(0, rows * 2 * units, depart, 0, unroll=4)
    for k in range(2):
        for i in range(rows):
            part = pl.ds(i, nq, stride=8)
            at = pl.ds(k * qp, nq)
            for which in range(2):
                disp_ref[which, k, part, :] = found[i, which, at, :]
                adv_wide[which, k, part, :] = found[i, 2 + which, at, :]
    adv_ref[...] = adv_wide[...].reshape(adv_ref.shape).astype(BF16)


def basis_table(total, lon_total):
    npairs = total // 2
    m = np.arange(npairs // 2, dtype=np.int64)
    j = np.arange(lon_total // 2, dtype=np.int64)
    orders = ((2 * m, total - 2 - 2 * m), (2 * m + 1, total - 1 - 2 * m))
    table = np.zeros((2, 2, 2, npairs // 2, lon_total // 2), np.float32)
    for parity in range(2):
        for half in range(2):
            order = orders[parity][half][:, None]
            angle = (2.0 * math.pi / lon_total) * ((order * j[None, :]) % lon_total)
            weight = np.where(order == 0, 1.0, 2.0)
            table[parity, half, 0] = weight * np.cos(angle)
            table[parity, half, 1] = -weight * np.sin(angle)
    return jnp.asarray(table.reshape(2, 2 * npairs, lon_total // 2).astype(BF16))


def depart_fields(sums, eta_shift, cells, nb, pairs, total):
    lon_total = eta_shift.shape[2]
    nq = lon_total // 128
    qp = -(-(nq + 2) // 8) * 8
    basis = basis_table(total, lon_total)
    window = -(-total // 4 // 128) * 128
    tiles = lambda a: jnp.swapaxes(a.reshape(a.shape[:-1] + (nq, 128)), -3, -2)
    eta = tiles(eta_shift)
    cells = tiles(cells).reshape(3, 2, nq * 8, 128)
    vmem = pl.BlockSpec(memory_space=pltpu.VMEM)
    anywhere = pl.BlockSpec(memory_space=pl.ANY)
    adv, disp = pl.pallas_call(
        functools.partial(fields_kernel, nb, nq, pairs),
        out_shape=(
            jax.ShapeDtypeStruct((2, 2, nq, 8, 128), BF16),
            jax.ShapeDtypeStruct((2, 2, nq * 8, 128), F32),
        ),
        in_specs=[anywhere] * 4,
        out_specs=(vmem, vmem),
        scratch_shapes=[
            pltpu.VMEM((nb * 16, 128), F32),
            pltpu.VMEM((nb * pairs, 9 * 128), BF16),
            pltpu.VMEM((nb * pairs, 2 * window), BF16),
            pltpu.VMEM((144, 8, 2 * window), F32),
            pltpu.VMEM((2, 4, 288, window), BF16),
            pltpu.VMEM(basis.shape, BF16),
            pltpu.VMEM((288 * qp + 8, 128), F32),
            pltpu.VMEM((12, 6, qp // 8, 2, 5, 16, 128), TAP),
            pltpu.VMEM(eta.shape, BF16),
            pltpu.VMEM(cells.shape, jnp.int32),
            pltpu.VMEM((8, 4, 2 * qp, 128), F32),
            pltpu.VMEM((nq * 8, 128), F32),
            pltpu.VMEM((8, 4, 2 * qp, 128), F32),
            pltpu.VMEM((2, 2, nq * 8, 128), F32),
            pltpu.VMEM(sums.shape, BF16),
            pltpu.SemaphoreType.DMA((-(-lon_total // 512),)),
            pltpu.SemaphoreType.DMA((2,)),
            pltpu.SemaphoreType.DMA((3,)),
        ],
        compiler_params=pltpu.CompilerParams(vmem_limit_bytes=VMEM_LIMIT),
        name="fields",
    )(sums, basis, eta, cells)
    whole = lambda a: jnp.swapaxes(a, -3, -2).reshape(2, 2, 8, lon_total)
    return whole(adv), whole(disp.reshape(2, 2, nq, 8, 128))


def per_device(spectra, legendre, pairing, eta_shift, cells):
    nb = legendre.shape[1]
    pairs, width = spectra.shape[2], spectra.shape[3]
    nx = lax.axis_size("lev") // 2
    sums = gather_sums(spectra, legendre, pairing, nb, nx)
    return depart_fields(sums, eta_shift, cells, nb, pairs, width - 1)


def solution(mesh):
    return jax.shard_map(
        per_device,
        mesh=mesh,
        in_specs=(
            P(None, "lev", "band", None),
            P("lev", None, "band", None),
            P("band"),
            P("lev", "band", None),
            P(None, "lev", "band", None),
        ),
        out_specs=(P(None, "lev", "band", None), P(None, "lev", "band", None)),
        check_vma=False,
    )
```

time: 67.2 us -> 56.6 us (0.84)
  Pallas kernels: 66.4 us -> 55.8 us
    pallas_call x1, Pallas kernels: 22.1 us -> 15.8 us  [depart_fields(): pl.pallas_call(functools.partial(fields_kernel, nb, nq, pairs), out_shape...]
    pallas_call x1, Pallas kernels: 44.3 us -> 40 us  [gather_sums(): pl.pallas_call(functools.partial(comm_kernel, nb, nx, pairs, width), out_...]
where the time goes in v2:
time: 56.6 us; the launch traced here: 56.4 us
  Pallas kernels  55.8 us (99%)
  between operations  0.64 us (1%)
    pallas_call x1, Pallas kernels, gather_sums(): pl.pallas_call(functools.partial(comm_kernel, nb, nx, pairs, width), out_...  40 us
    pallas_call x1, Pallas kernels, depart_fields(): pl.pallas_call(functools.partial(fields_kernel, nb, nq, pairs), out_shape...  15.8 us

profile of v2, /device:TPU:1, one launch (start us, length us, event | category | flops | bytes accessed | tf_op | source)
XLA Modules:
  0.0 56.4 jit_solution(6667064689628513272)
XLA Ops:
  0.6 40.0 %sums.1.sums_hbm = bf16[3,64,16,128]{3,2,1,0:T(8,128)(2,1)} custom-call(bf16[2,5,8,641]{3,2,1,0:T(8,128)(2,1)} %bitcast.22, bf16[5,64,641]{2,1,0:T(8,128)(2,1)} %bitcast.21, s32[5]{0:T(128)} %pair_ref.1), custom_call_target="tpu_custom_call" | custom-call | tf_op jit(solution)/shard_map/sums/pallas_call | solution.py:296
  40.7 15.8 %fields.1 = (bf16[2,2,22,8,128]{4,3,2,1,0:T(8,128)(2,1)}, f32[2,2,176,128]{3,2,1,0:T(8,128)}) custom-call(bf16[3,64,16,128]{3,2,1,0:T(8,128)(2,1)} %sums.1.sums_hbm, bf16[2,640,1408]{2,1,0:T(8,128)(2,1)} %constant.2.clone.basis_ref, bf16[2,22,8,128]{3,2,1,0:T(8,128)(2,1)} %bitcast.23, s32[3,2,176,128]{3,2,1,0:T(8,128)} %bitcast.20), custom_call_target="tpu_custom_call" | custom-call | tf_op jit(solution)/shard_map/fields/pallas_call | solution.py:593

commit v3 on v2

--- a/solution.py
+++ b/solution.py
@@ -27,15 +27,19 @@
     return lax.dot_general(a, b, (((0,), (0,)), ((), ())), preferred_element_type=F32)
 
 
-def comm_kernel(
+def gather_sums(
     nb,
     nx,
     pairs,
     width,
+    after_sums,
+    after_sends,
+    after_own,
     spec_ref,
     leg_ref,
     pair_ref,
-    out_ref,
+    recv,
+    halo,
     raw,
     specg,
     last,
@@ -44,8 +48,6 @@
     sums_in,
     stage,
     send,
-    recv,
-    nothing,
     load_sem,
     last_send,
     last_recv,
@@ -59,7 +61,6 @@
     band_recv,
     halo_send,
     halo_recv,
-    own_sem,
     lev_ready,
     band_ready,
 ):
@@ -136,7 +137,7 @@
 
     for d in order:
         signal(barrier, lax.rem(b + d, nb), 2 * x + 1)
-    nothing[...] = jnp.zeros(nothing.shape, BF16)
+    after_sums()
 
     columns = lax.broadcasted_iota(jnp.int32, (16, width - 1), 1)
     zero = jnp.zeros((16, width - 1), F32)
@@ -219,17 +220,16 @@
 
     above = (b, lax.rem(lev + 1, nlev))
     below = (b, lax.rem(lev + nlev - 1, nlev))
-    lowest = lev == 0
-    highest = lev == nlev - 1
-
-    @pl.when(lowest)
-    def _():
-        pltpu.make_async_copy(nothing, out_ref.at[0], own_sem.at[0]).start()
-
-    @pl.when(highest)
-    def _():
-        pltpu.make_async_copy(nothing, out_ref.at[2], own_sem.at[0]).start()
-
+
+    @pl.when(lev == 0)
+    def _():
+        halo[0] = jnp.zeros(recv.shape, BF16)
+
+    @pl.when(lev == nlev - 1)
+    def _():
+        halo[1] = jnp.zeros(recv.shape, BF16)
+
+    after_sends()
     for g in reversed(range(GROUPS)):
         end = min(nb - 1, (g + 1) * group)
         if end > g * group:
@@ -240,18 +240,16 @@
         @pl.when(lev < nlev - 1)
         def _():
             remote(
-                recv.at[part], out_ref.at[0, part], halo_send.at[0], halo_recv.at[0], *above
+                recv.at[part], halo.at[0, part], halo_send.at[0], halo_recv.at[0], *above
             ).start()
 
         @pl.when(lev > 0)
         def _():
             remote(
-                recv.at[part], out_ref.at[2, part], halo_send.at[1], halo_recv.at[1], *below
+                recv.at[part], halo.at[1, part], halo_send.at[1], halo_recv.at[1], *below
             ).start()
 
-    own = pltpu.make_async_copy(recv, out_ref.at[1], own_sem.at[1])
-    own.start()
-
+    after_own()
     others = last.at[pl.ds(1, nx - 1)]
     remote(others, others, last_send, last_recv, *sibling).wait_send()
     others = specg.at[:, pl.ds(1, nx - 1)]
@@ -262,10 +260,9 @@
     remote(others, others, x_send, x_recv.at[0], *sibling).wait_send()
     arrived = recv.at[pl.ds(0, nb - 1)]
     remote(arrived, arrived, band_send, band_recv.at[0], *sibling).wait_send()
-    own.wait()
-
-    up = remote(recv, out_ref.at[0], halo_send.at[0], halo_recv.at[0], *above)
-    down = remote(recv, out_ref.at[2], halo_send.at[1], halo_recv.at[1], *below)
+
+    up = remote(recv, halo.at[0], halo_send.at[0], halo_recv.at[0], *above)
+    down = remote(recv, halo.at[1], halo_send.at[1], halo_recv.at[1], *below)
 
     @pl.when(lev > 0)
     def _():
@@ -276,61 +273,6 @@
     def _():
         down.wait_recv()
         up.wait_send()
-
-    @pl.when(lowest)
-    def _():
-        pltpu.make_async_copy(nothing, out_ref.at[0], own_sem.at[0]).wait()
-
-    @pl.when(highest)
-    def _():
-        pltpu.make_async_copy(nothing, out_ref.at[2], own_sem.at[0]).wait()
-
-
-def gather_sums(spectra, legendre, pairing, nb, nx):
-    pairs, width = spectra.shape[2], spectra.shape[3]
-    spec = jnp.transpose(spectra, (0, 2, 1, 3))
-    table = jnp.transpose(legendre[0], (1, 0, 2))
-    lanes = nx * 32
-    dma = pltpu.SemaphoreType.DMA
-    anywhere = pl.BlockSpec(memory_space=pl.ANY)
-    return pl.pallas_call(
-        functools.partial(comm_kernel, nb, nx, pairs, width),
-        out_shape=jax.ShapeDtypeStruct((3, nb, 16, lanes), BF16),
-        in_specs=[anywhere, anywhere, pl.BlockSpec(memory_space=pltpu.SMEM)],
-        out_specs=anywhere,
-        scratch_shapes=[
-            pltpu.VMEM(spec.shape, BF16),
-            pltpu.VMEM((pairs, nx, 16, width - 1), BF16),
-            pltpu.VMEM((nx, 16, 128), BF16),
-            pltpu.VMEM((pairs, 2, nb, width), BF16),
-            pltpu.VMEM((pairs, nx, 32, 2 * nb), BF16),
-            pltpu.VMEM((pairs, nx, 32, 2 * nb), BF16),
-            pltpu.VMEM((nb * 16, lanes), F32),
-            pltpu.VMEM((nb, 16, lanes), BF16),
-            pltpu.VMEM((nb, 16, lanes), BF16),
-            pltpu.VMEM((nb, 16, lanes), BF16),
-            dma((2,)),
-            dma,
-            dma,
-            dma,
-            dma((pairs,)),
-            dma,
-            dma((pairs,)),
-            dma,
-            dma((pairs,)),
-            dma,
-            dma((GROUPS,)),
-            dma((2,)),
-            dma((2,)),
-            dma((2,)),
-            pltpu.SemaphoreType.REGULAR,
-            pltpu.SemaphoreType.REGULAR,
-        ],
-        compiler_params=pltpu.CompilerParams(
-            collective_id=0, has_side_effects=True, vmem_limit_bytes=VMEM_LIMIT
-        ),
-        name="sums",
-    )(spec, table, pairing)
 
 
 def lagrange_taps(shift, back):
@@ -359,11 +301,15 @@
     return total
 
 
-def fields_kernel(
+def whole_kernel(
     nb,
+    nx,
     nq,
     pairs,
-    sums_hbm,
+    width,
+    spec_ref,
+    leg_ref,
+    pair_ref,
     basis_ref,
     eta_ref,
     cells_ref,
@@ -383,10 +329,11 @@
     eta_wide,
     found,
     adv_wide,
-    sums_ref,
     basis_sem,
     point_sem,
-    sums_sem,
+    recv,
+    halo,
+    *rest,
 ):
     qp = grid.shape[0] // 8 * 8 // 288
     half = nb * pairs // 2
@@ -397,72 +344,120 @@
     row0 = lax.axis_index("band") * rows
     lev0 = lax.axis_index("lev") * 2
 
-    sums_copies = [
-        pltpu.make_async_copy(sums_hbm.at[g], sums_ref.at[g], sums_sem.at[g]) for g in range(3)
+    blocks = [(start, min(256, lon_half - start)) for start in range(0, lon_half, 256)]
+    basis_copies = [
+        pltpu.make_async_copy(
+            basis_ref.at[:, :, pl.ds(start, size)],
+            basis.at[:, :, pl.ds(start, size)],
+            basis_sem.at[n],
+        )
+        for n, (start, size) in enumerate(blocks)
     ]
-    for copy in sums_copies:
-        copy.start()
-    blocks = [(start, min(256, lon_half - start)) for start in range(0, lon_half, 256)]
-    basis_copies = []
-    for n, (start, size) in enumerate(blocks):
-        part = pl.ds(start, size)
-        copy = pltpu.make_async_copy(
-            basis_ref.at[:, :, part], basis.at[:, :, part], basis_sem.at[n]
-        )
-        copy.start()
-        basis_copies.append(copy)
     point_copies = (
         pltpu.make_async_copy(eta_ref, eta, point_sem.at[0]),
         pltpu.make_async_copy(cells_ref, cells, point_sem.at[1]),
     )
-    for copy in point_copies:
-        copy.start()
-
-    for g in range(3):
-        sums_copies[g].wait()
-        wide[...] = sums_ref[g].astype(F32).reshape(nb * 16, 128)
-        for p in range(pairs):
-            for t, at in enumerate((2 * p, 2 * p + 1, 2 * pairs + p)):
-                slots[p * nb : (p + 1) * nb, (g * 3 + t) * 128 : (g * 3 + t + 1) * 128] = wide[
-                    pl.ds(at, nb, stride=16), :
-                ].astype(BF16)
-        if g == 1:
-            numbers = wide[pl.ds(3 * pairs, nb, stride=16), :].astype(jnp.int32)
-            column = lax.broadcasted_iota(jnp.int32, (nb, 2 * window), 1)
-            order = jnp.where(column < window, 2 * column, 2 * (column - window) + 1)
+
+    def start_copies():
+        for copy in (*point_copies, *basis_copies):
+            copy.start()
+
+    def read_points():
+        for copy in (*point_copies, *basis_copies):
+            copy.wait()
+        lon = (
+            lax.broadcasted_iota(jnp.int32, (nq, 128), 0) * 128
+            + lax.broadcasted_iota(jnp.int32, (nq, 128), 1)
+        )
+        for k in range(2):
+            eta_wide[...] = eta[k].astype(F32).reshape(nq * 8, 128)
+            for i in range(rows):
+                part = pl.ds(i, nq, stride=8)
+                at = pl.ds(k * qp, nq)
+                points[i, 0, at, :] = jnp.where(cells[0, k, part, :] == row0 + i, 0.0, 1.0)
+                points[i, 1, at, :] = jnp.where(cells[1, k, part, :] == lon, 0.0, 1.0)
+                points[i, 2, at, :] = jnp.where(cells[2, k, part, :] == lev0 + k, 0.0, 1.0)
+                points[i, 3, at, :] = eta_wide[part, :]
+
+    def synthesise(groups, place_of, sums_of):
+        first, count = place_of[groups[0]], len(groups)
+        for g in groups:
+            wide[...] = sums_of[g].astype(F32).reshape(nb * 16, 128)
             for p in range(pairs):
-                number = numbers[:, 2 * p : 2 * p + 1] * 128 + numbers[:, 2 * p + 1 : 2 * p + 2]
-                place[p * nb : (p + 1) * nb, :] = jnp.where(order == number, 1.0, 0.0).astype(BF16)
-    orders[...] = tn_dot(slots[...], place[...]).reshape(144, 8, 2 * window)
-    for parity in range(2):
-        for part in range(4):
-            first = window * ((part // 2 + parity) % 2)
-            coef[parity, part] = jnp.concatenate(
-                [orders[4 * m + part, :, first : first + window] for m in range(36)], axis=0
-            ).astype(BF16)
-
-    for (start, size), copy in zip(blocks, basis_copies):
-        copy.wait()
-        even, odd = [
-            sum(
-                jnp.dot(
-                    coef[parity, part, :, :half],
-                    basis[parity, part * half : (part + 1) * half, start : start + size],
-                    preferred_element_type=F32,
+                for t, at in enumerate((2 * p, 2 * p + 1, 2 * pairs + p)):
+                    lanes = (place_of[g] * 3 + t) * 128
+                    slots[p * nb : (p + 1) * nb, lanes : lanes + 128] = wide[
+                        pl.ds(at, nb, stride=16), :
+                    ].astype(BF16)
+            if g == 1:
+                numbers = wide[pl.ds(3 * pairs, nb, stride=16), :].astype(jnp.int32)
+                column = lax.broadcasted_iota(jnp.int32, (nb, 2 * window), 1)
+                order = jnp.where(column < window, 2 * column, 2 * (column - window) + 1)
+                for p in range(pairs):
+                    number = (
+                        numbers[:, 2 * p : 2 * p + 1] * 128 + numbers[:, 2 * p + 1 : 2 * p + 2]
+                    )
+                    place[p * nb : (p + 1) * nb, :] = jnp.where(order == number, 1.0, 0.0).astype(
+                        BF16
+                    )
+        used = slots[:, first * 384 : (first + count) * 384]
+        orders[first * 48 : (first + count) * 48] = tn_dot(used, place[...]).reshape(
+            count * 48, 8, 2 * window
+        )
+        lines = pl.ds(first * 96, count * 96)
+        for parity in range(2):
+            for part in range(4):
+                start = window * ((part // 2 + parity) % 2)
+                coef[parity, part, lines, :] = jnp.concatenate(
+                    [
+                        orders[first * 48 + 4 * m + part, :, start : start + window]
+                        for m in range(12 * count)
+                    ],
+                    axis=0,
+                ).astype(BF16)
+        for start, size in blocks:
+            even, odd = [
+                sum(
+                    jnp.dot(
+                        coef[parity, part, lines, :half],
+                        basis[parity, part * half : (part + 1) * half, start : start + size],
+                        preferred_element_type=F32,
+                    )
+                    for part in range(4)
                 )
-                for part in range(4)
-            )
-            for parity in range(2)
-        ]
-        for turn, values in enumerate((even + odd, even - odd)):
-            for m in range(36):
-                g, t, xs = m // 12, (m // 4) % 3, m % 4
-                row = 2 + 2 * xs + t if t < 2 else (xs // 2 + (xs % 2) * 10)
-                base = (row * 3 + g) * 8 * qp + 1 + (start + turn * lon_half) // 128
-                for w in range(size // 128):
-                    grid[pl.ds(base + w, 8, stride=qp), :] = values[
-                        m * 8 : (m + 1) * 8, w * 128 : (w + 1) * 128
-                    ]
+                for parity in range(2)
+            ]
+            for turn, values in enumerate((even + odd, even - odd)):
+                for m in range(12 * count):
+                    g, t, xs = groups[m // 12], (m // 4) % 3, m % 4
+                    row = 2 + 2 * xs + t if t < 2 else (xs // 2 + (xs % 2) * 10)
+                    base = (row * 3 + g) * 8 * qp + 1 + (start + turn * lon_half) // 128
+                    for w in range(size // 128):
+                        grid[pl.ds(base + w, 8, stride=qp), :] = values[
+                            m * 8 : (m + 1) * 8, w * 128 : (w + 1) * 128
+                        ]
+
+    place_of = (1, 0, 2)
+
+    def own_levels():
+        synthesise((1,), place_of, {1: recv[...]})
+
+    gather_sums(
+        nb,
+        nx,
+        pairs,
+        width,
+        start_copies,
+        read_points,
+        own_levels,
+        spec_ref,
+        leg_ref,
+        pair_ref,
+        recv,
+        halo,
+        *rest,
+    )
+    synthesise((0, 2), place_of, {0: halo[0], 2: halo[1]})
     grid[pl.ds(0, 288, stride=qp), :] = grid[pl.ds(nq, 288, stride=qp), :]
     grid[pl.ds(nq + 1, 288, stride=qp), :] = grid[pl.ds(1, 288, stride=qp), :]
 
@@ -494,22 +489,6 @@
         return carry
 
     lax.fori_loop(0, 72, shift_fields, 0, unroll=8)
-
-    for copy in point_copies:
-        copy.wait()
-    for k in range(2):
-        eta_wide[...] = eta[k].astype(F32).reshape(nq * 8, 128)
-        lon = (
-            lax.broadcasted_iota(jnp.int32, (nq, 128), 0) * 128
-            + lax.broadcasted_iota(jnp.int32, (nq, 128), 1)
-        )
-        for i in range(rows):
-            part = pl.ds(i, nq, stride=8)
-            at = pl.ds(k * qp, nq)
-            points[i, 0, at, :] = jnp.where(cells[0, k, part, :] == row0 + i, 0.0, 1.0)
-            points[i, 1, at, :] = jnp.where(cells[1, k, part, :] == lon, 0.0, 1.0)
-            points[i, 2, at, :] = jnp.where(cells[2, k, part, :] == lev0 + k, 0.0, 1.0)
-            points[i, 3, at, :] = eta_wide[part, :]
 
     def double(taps):
         return [jnp.concatenate([tap, tap], axis=0).astype(TAP) for tap in taps]
@@ -579,24 +558,37 @@
     return jnp.asarray(table.reshape(2, 2 * npairs, lon_total // 2).astype(BF16))
 
 
-def depart_fields(sums, eta_shift, cells, nb, pairs, total):
+def hand_over(adv_ref, disp_ref, adv_out, disp_out):
+    adv_out[...] = adv_ref[...]
+    disp_out[...] = disp_ref[...]
+
+
+def per_device(spectra, legendre, pairing, eta_shift, cells):
+    nb = legendre.shape[1]
+    pairs, width = spectra.shape[2], spectra.shape[3]
+    nx = lax.axis_size("lev") // 2
     lon_total = eta_shift.shape[2]
     nq = lon_total // 128
     qp = -(-(nq + 2) // 8) * 8
-    basis = basis_table(total, lon_total)
-    window = -(-total // 4 // 128) * 128
+    basis = basis_table(width - 1, lon_total)
+    window = -(-(width - 1) // 4 // 128) * 128
     tiles = lambda a: jnp.swapaxes(a.reshape(a.shape[:-1] + (nq, 128)), -3, -2)
     eta = tiles(eta_shift)
     cells = tiles(cells).reshape(3, 2, nq * 8, 128)
+    spec = jnp.transpose(spectra, (0, 2, 1, 3))
+    table = jnp.transpose(legendre[0], (1, 0, 2))
+    lanes = nx * 32
+    dma = pltpu.SemaphoreType.DMA
+    regular = pltpu.SemaphoreType.REGULAR
     vmem = pl.BlockSpec(memory_space=pltpu.VMEM)
     anywhere = pl.BlockSpec(memory_space=pl.ANY)
     adv, disp = pl.pallas_call(
-        functools.partial(fields_kernel, nb, nq, pairs),
+        functools.partial(whole_kernel, nb, nx, nq, pairs, width),
         out_shape=(
             jax.ShapeDtypeStruct((2, 2, nq, 8, 128), BF16),
             jax.ShapeDtypeStruct((2, 2, nq * 8, 128), F32),
         ),
-        in_specs=[anywhere] * 4,
+        in_specs=[anywhere, anywhere, pl.BlockSpec(memory_space=pltpu.SMEM)] + [anywhere] * 3,
         out_specs=(vmem, vmem),
         scratch_shapes=[
             pltpu.VMEM((nb * 16, 128), F32),
@@ -613,24 +605,51 @@
             pltpu.VMEM((nq * 8, 128), F32),
             pltpu.VMEM((8, 4, 2 * qp, 128), F32),
             pltpu.VMEM((2, 2, nq * 8, 128), F32),
-            pltpu.VMEM(sums.shape, BF16),
-            pltpu.SemaphoreType.DMA((-(-lon_total // 512),)),
-            pltpu.SemaphoreType.DMA((2,)),
-            pltpu.SemaphoreType.DMA((3,)),
+            dma((-(-lon_total // 512),)),
+            dma((2,)),
+            pltpu.VMEM((nb, 16, lanes), BF16),
+            pltpu.VMEM((2, nb, 16, lanes), BF16),
+            pltpu.VMEM(spec.shape, BF16),
+            pltpu.VMEM((pairs, nx, 16, width - 1), BF16),
+            pltpu.VMEM((nx, 16, 128), BF16),
+            pltpu.VMEM((pairs, 2, nb, width), BF16),
+            pltpu.VMEM((pairs, nx, 32, 2 * nb), BF16),
+            pltpu.VMEM((pairs, nx, 32, 2 * nb), BF16),
+            pltpu.VMEM((nb * 16, lanes), F32),
+            pltpu.VMEM((nb, 16, lanes), BF16),
+            dma((2,)),
+            dma,
+            dma,
+            dma,
+            dma((pairs,)),
+            dma,
+            dma((pairs,)),
+            dma,
+            dma((pairs,)),
+            dma,
+            dma((GROUPS,)),
+            dma((2,)),
+            dma((2,)),
+            regular,
+            regular,
         ],
-        compiler_params=pltpu.CompilerParams(vmem_limit_bytes=VMEM_LIMIT),
-        name="fields",
-    )(sums, basis, eta, cells)
+        compiler_params=pltpu.CompilerParams(
+            collective_id=0, has_side_effects=True, vmem_limit_bytes=VMEM_LIMIT
+        ),
+        name="winds",
+    )(spec, table, pairing, basis, eta, cells)
+    adv, disp = pl.pallas_call(
+        hand_over,
+        out_shape=(
+            jax.ShapeDtypeStruct(adv.shape, adv.dtype),
+            jax.ShapeDtypeStruct(disp.shape, disp.dtype),
+        ),
+        in_specs=[vmem] * 2,
+        out_specs=(vmem, vmem),
+        name="results",
+    )(adv, disp)
     whole = lambda a: jnp.swapaxes(a, -3, -2).reshape(2, 2, 8, lon_total)
     return whole(adv), whole(disp.reshape(2, 2, nq, 8, 128))
-
-
-def per_device(spectra, legendre, pairing, eta_shift, cells):
-    nb = legendre.shape[1]
-    pairs, width = spectra.shape[2], spectra.shape[3]
-    nx = lax.axis_size("lev") // 2
-    sums = gather_sums(spectra, legendre, pairing, nb, nx)
-    return depart_fields(sums, eta_shift, cells, nb, pairs, width - 1)
 
 
 def solution(mesh):

time: 56.6 us -> 54.6 us (0.965)
  Pallas kernels: 55.8 us -> 53.8 us
    pallas_call x2, Pallas kernels: 55.8 us -> 53.8 us  [the longest x1 51.9 us: per_device(): pl.pallas_call(functools.partial(whole_kernel, nb, nx, nq, pairs, width),...]
where the time goes in v3:
time: 54.6 us; the launch traced here: 54.4 us
  Pallas kernels  53.8 us (99%)
  between operations  0.64 us (1%)
    pallas_call x1, Pallas kernels, per_device(): pl.pallas_call(functools.partial(whole_kernel, nb, nx, nq, pairs, width),...  51.9 us
    pallas_call x1, Pallas kernels, per_device(): pl.pallas_call(hand_over, out_shape=(jax.ShapeDtypeStruct(adv.shape, adv....  1.89 us

profile of v3, /device:TPU:1, one launch (start us, length us, event | category | flops | bytes accessed | tf_op | source)
XLA Modules:
  0.0 54.4 jit_solution(15158257014229171896)
XLA Ops:
  0.6 51.9 %winds.1 = (bf16[2,2,22,8,128]{4,3,2,1,0:T(8,128)(2,1)}, f32[2,2,176,128]{3,2,1,0:T(8,128)}) custom-call(bf16[2,5,8,641]{3,2,1,0:T(8,128)(2,1)} %bitcast.22, bf16[5,64,641]{2,1,0:T(8,128)(2,1)} %bitcast.21, s32[5]{0:T(128)} %pair_ref.1, bf16[2,640,1408]{2,1,0:T(8,128)(2,1)} %constant.2.clone.basis_ref, bf16[2,22,8,128]{3,2,1,0:T(8,128)(2,1)} %bitcast.23, ...), custom_call_target="tpu_custom_call" | custom-call | tf_op jit(solution)/shard_map/winds/pallas_call | solution.py:585
  52.5 1.9 %results.1 = (bf16[2,2,22,8,128]{4,3,2,1,0:T(8,128)(2,1)}, f32[2,2,176,128]{3,2,1,0:T(8,128)}) custom-call(bf16[2,2,22,8,128]{4,3,2,1,0:T(8,128)(2,1)} %get-tuple-element.6.adv_ref, f32[2,2,176,128]{3,2,1,0:T(8,128)} %get-tuple-element.7.disp_ref), custom_call_target="tpu_custom_call" | custom-call | tf_op jit(solution)/shard_map/results/pallas_call | solution.py:641

commit v4 on v3

--- a/solution.py
+++ b/solution.py
@@ -107,6 +107,8 @@
     def _():
         signal(barrier, b, 2 * x)
 
+    for d in order:
+        signal(barrier, lax.rem(b + d, nb), 2 * x + 1)
     loads[0].wait()
     tail = jnp.zeros((16, 128), F32)
     place = lax.broadcasted_iota(jnp.int32, (16, 128), 1)
@@ -135,8 +137,6 @@
             loads[1].wait()
         remote(legs.at[p, core], legs.at[p, core], leg_send, leg_recv.at[p], *sibling).start()
 
-    for d in order:
-        signal(barrier, lax.rem(b + d, nb), 2 * x + 1)
     after_sums()
 
     columns = lax.broadcasted_iota(jnp.int32, (16, width - 1), 1)
@@ -327,10 +327,12 @@
     cells,
     points,
     eta_wide,
-    found,
+    disp,
     adv_wide,
+    adv,
     basis_sem,
     point_sem,
+    out_sem,
     recv,
     halo,
     *rest,
@@ -378,6 +380,36 @@
                 points[i, 1, at, :] = jnp.where(cells[1, k, part, :] == lon, 0.0, 1.0)
                 points[i, 2, at, :] = jnp.where(cells[2, k, part, :] == lev0 + k, 0.0, 1.0)
                 points[i, 3, at, :] = eta_wide[part, :]
+
+    lane = lax.broadcasted_iota(jnp.int32, (16, 128), 1).astype(F32).astype(TAP)
+    inside = {c: (lane >= c if c > 0 else lane < 128 + c) for c in (-2, -1, 1, 2)}
+
+    def shift_fields(first, count, n, carry):
+        row, level = n // count, first + n % count
+        if count == 4:
+            level = level + 2 * (n % count // 2)
+        at = (row * 6 + level) * 4
+        for two in range(2):
+            for t in range(units):
+
+                def block(offset):
+                    return jnp.concatenate(
+                        [
+                            grid[pl.ds((at + field) * qp + 8 * t + offset, 8), :]
+                            for field in (2 * two, 2 * two + 1)
+                        ],
+                        axis=0,
+                    ).astype(TAP)
+
+                ahead, here, after = block(0), block(1), block(2)
+                for c in range(-2, 3):
+                    value = here
+                    if c > 0:
+                        value = pltpu.roll(jnp.where(inside[c], here, after), 128 - c, 1)
+                    elif c < 0:
+                        value = pltpu.roll(jnp.where(inside[c], here, ahead), -c, 1)
+                    near[row, level, t, two, c + 2] = value
+        return carry
 
     def synthesise(groups, place_of, sums_of):
         first, count = place_of[groups[0]], len(groups)
@@ -436,6 +468,15 @@
                         grid[pl.ds(base + w, 8, stride=qp), :] = values[
                             m * 8 : (m + 1) * 8, w * 128 : (w + 1) * 128
                         ]
+        for row in range(12):
+            for g in groups:
+                base = (row * 3 + g) * 8 * qp
+                for target, source in ((0, nq), (nq + 1, 1)):
+                    grid[pl.ds(base + target, 8, stride=qp), :] = grid[
+                        pl.ds(base + source, 8, stride=qp), :
+                    ]
+        shift = functools.partial(shift_fields, 2 * groups[0], 2 * count)
+        lax.fori_loop(0, 24 * count, shift, 0, unroll=12)
 
     place_of = (1, 0, 2)
 
@@ -458,43 +499,10 @@
         *rest,
     )
     synthesise((0, 2), place_of, {0: halo[0], 2: halo[1]})
-    grid[pl.ds(0, 288, stride=qp), :] = grid[pl.ds(nq, 288, stride=qp), :]
-    grid[pl.ds(nq + 1, 288, stride=qp), :] = grid[pl.ds(1, 288, stride=qp), :]
-
-    lane = lax.broadcasted_iota(jnp.int32, (16, 128), 1).astype(F32).astype(TAP)
-    inside = {c: (lane >= c if c > 0 else lane < 128 + c) for c in (-2, -1, 1, 2)}
-
-    def shift_fields(n, carry):
-        row, level = n // 6, n % 6
-        for two in range(2):
-            for t in range(units):
-
-                def block(offset):
-                    return jnp.concatenate(
-                        [
-                            grid[pl.ds((n * 4 + field) * qp + 8 * t + offset, 8), :]
-                            for field in (2 * two, 2 * two + 1)
-                        ],
-                        axis=0,
-                    ).astype(TAP)
-
-                ahead, here, after = block(0), block(1), block(2)
-                for c in range(-2, 3):
-                    value = here
-                    if c > 0:
-                        value = pltpu.roll(jnp.where(inside[c], here, after), 128 - c, 1)
-                    elif c < 0:
-                        value = pltpu.roll(jnp.where(inside[c], here, ahead), -c, 1)
-                    near[row, level, t, two, c + 2] = value
-        return carry
-
-    lax.fori_loop(0, 72, shift_fields, 0, unroll=8)
-
     def double(taps):
         return [jnp.concatenate([tap, tap], axis=0).astype(TAP) for tap in taps]
 
-    def depart(n, carry):
-        i, k, t = n // (2 * units), (n // units) % 2, n % units
+    def depart(k, t, i, carry):
         at = pl.ds(pl.multiple_of((k * units + t) * 8, 8), 8)
         row_back, lon_back = points[i, 0, at, :], points[i, 1, at, :]
         level_taps = double(lagrange_taps(points[i, 3, at, :], points[i, 2, at, :]))
@@ -524,22 +532,45 @@
             east_found, north_found = horizontal(wind_sums, shift_row, shift_lon)
             shift_row = 0.5 * COURANT * (north + north_found)
             shift_lon = 0.5 * COURANT * (east + east_found)
-        found[i, 0, at, :] = shift_row
-        found[i, 1, at, :] = shift_lon
         heat, moisture = horizontal(level_sums(1), shift_row, shift_lon)
-        found[i, 2, at, :] = heat
-        found[i, 3, at, :] = moisture
+        out = pl.ds(t * 64 + i, 8, stride=8)
+        disp[0, k, out, :] = shift_row
+        disp[1, k, out, :] = shift_lon
+        adv_wide[0, k, out, :] = heat
+        adv_wide[1, k, out, :] = moisture
         return carry
 
-    lax.fori_loop(0, rows * 2 * units, depart, 0, unroll=4)
-    for k in range(2):
-        for i in range(rows):
-            part = pl.ds(i, nq, stride=8)
-            at = pl.ds(k * qp, nq)
-            for which in range(2):
-                disp_ref[which, k, part, :] = found[i, which, at, :]
-                adv_wide[which, k, part, :] = found[i, 2 + which, at, :]
-    adv_ref[...] = adv_wide[...].reshape(adv_ref.shape).astype(BF16)
+    def results(k, t, size):
+        for which in range(2):
+            blocks = pl.ds(t * 8, size)
+            lines = pl.ds(pl.multiple_of(t * 64, 64), size * 8)
+            adv[which, k, blocks] = (
+                adv_wide[which, k, lines, :].reshape(size, 8, 128).astype(BF16)
+            )
+            pltpu.make_async_copy(
+                adv.at[which, k, blocks], adv_ref.at[which, k, blocks], out_sem.at[0]
+            ).start()
+            pltpu.make_async_copy(
+                disp.at[which, k, lines], disp_ref.at[which, k, lines], out_sem.at[1]
+            ).start()
+
+    def depart_block(n, carry):
+        k, t = n // units, n % units
+        lax.fori_loop(0, rows, functools.partial(depart, k, t), 0, unroll=8)
+
+        @pl.when(t < units - 1)
+        def _():
+            results(k, t, 8)
+
+        @pl.when(t == units - 1)
+        def _():
+            results(k, t, nq - 8 * (units - 1))
+
+        return carry
+
+    lax.fori_loop(0, 2 * units, depart_block, 0)
+    pltpu.make_async_copy(adv.at[:, :, pl.ds(0, nq)], adv_ref, out_sem.at[0]).wait()
+    pltpu.make_async_copy(disp.at[:, :, pl.ds(0, nq * 8)], disp_ref, out_sem.at[1]).wait()
 
 
 def basis_table(total, lon_total):
@@ -558,9 +589,27 @@
     return jnp.asarray(table.reshape(2, 2 * npairs, lon_total // 2).astype(BF16))
 
 
-def hand_over(adv_ref, disp_ref, adv_out, disp_out):
-    adv_out[...] = adv_ref[...]
-    disp_out[...] = disp_ref[...]
+def hand_over(adv_ref, disp_ref, adv_out, disp_out, adv, disp, in_sem, out_sem):
+    steps = []
+    for n, (source, held, target) in enumerate(
+        ((disp_ref, disp, disp_out), (adv_ref, adv, adv_out))
+    ):
+        for which in range(2):
+            for k in range(2):
+                at = (n, which, k)
+                inward = pltpu.make_async_copy(
+                    source.at[which, k], held.at[which, k], in_sem.at[at]
+                )
+                outward = pltpu.make_async_copy(
+                    held.at[which, k], target.at[which, k], out_sem.at[at]
+                )
+                inward.start()
+                steps.append((inward, outward))
+    for inward, outward in steps:
+        inward.wait()
+        outward.start()
+    for inward, outward in steps:
+        outward.wait()
 
 
 def per_device(spectra, legendre, pairing, eta_shift, cells):
@@ -580,7 +629,6 @@
     lanes = nx * 32
     dma = pltpu.SemaphoreType.DMA
     regular = pltpu.SemaphoreType.REGULAR
-    vmem = pl.BlockSpec(memory_space=pltpu.VMEM)
     anywhere = pl.BlockSpec(memory_space=pl.ANY)
     adv, disp = pl.pallas_call(
         functools.partial(whole_kernel, nb, nx, nq, pairs, width),
@@ -589,7 +637,7 @@
             jax.ShapeDtypeStruct((2, 2, nq * 8, 128), F32),
         ),
         in_specs=[anywhere, anywhere, pl.BlockSpec(memory_space=pltpu.SMEM)] + [anywhere] * 3,
-        out_specs=(vmem, vmem),
+        out_specs=(anywhere, anywhere),
         scratch_shapes=[
             pltpu.VMEM((nb * 16, 128), F32),
             pltpu.VMEM((nb * pairs, 9 * 128), BF16),
@@ -603,9 +651,11 @@
             pltpu.VMEM(cells.shape, jnp.int32),
             pltpu.VMEM((8, 4, 2 * qp, 128), F32),
             pltpu.VMEM((nq * 8, 128), F32),
-            pltpu.VMEM((8, 4, 2 * qp, 128), F32),
-            pltpu.VMEM((2, 2, nq * 8, 128), F32),
+            pltpu.VMEM((2, 2, qp * 8, 128), F32),
+            pltpu.VMEM((2, 2, qp * 8, 128), F32),
+            pltpu.VMEM((2, 2, qp, 8, 128), BF16),
             dma((-(-lon_total // 512),)),
+            dma((2,)),
             dma((2,)),
             pltpu.VMEM((nb, 16, lanes), BF16),
             pltpu.VMEM((2, nb, 16, lanes), BF16),
@@ -644,8 +694,14 @@
             jax.ShapeDtypeStruct(adv.shape, adv.dtype),
             jax.ShapeDtypeStruct(disp.shape, disp.dtype),
         ),
-        in_specs=[vmem] * 2,
-        out_specs=(vmem, vmem),
+        in_specs=[anywhere] * 2,
+        out_specs=(anywhere, anywhere),
+        scratch_shapes=[
+            pltpu.VMEM(adv.shape, adv.dtype),
+            pltpu.VMEM(disp.shape, disp.dtype),
+            dma((2, 2, 2)),
+            dma((2, 2, 2)),
+        ],
         name="results",
     )(adv, disp)
     whole = lambda a: jnp.swapaxes(a, -3, -2).reshape(2, 2, 8, lon_total)

time: 54.6 us -> 53.1 us (0.973)
  Pallas kernels: 53.8 us -> 52.2 us
    pallas_call x1, Pallas kernels: 51.9 us -> 50.4 us  [per_device(): pl.pallas_call(functools.partial(whole_kernel, nb, nx, nq, pairs, width),...]
where the time goes in v4:
time: 53.1 us; the launch traced here: 52.9 us
  Pallas kernels  52.2 us (98%)
  between operations  0.64 us (1%)
    pallas_call x1, Pallas kernels, per_device(): pl.pallas_call(functools.partial(whole_kernel, nb, nx, nq, pairs, width),...  50.4 us
    pallas_call x1, Pallas kernels, per_device(): pl.pallas_call(hand_over, out_shape=(jax.ShapeDtypeStruct(adv.shape, adv....  1.85 us

profile of v4, /device:TPU:1, one launch (start us, length us, event | category | flops | bytes accessed | tf_op | source)
XLA Modules:
  0.0 52.9 jit_solution(14532871182679146115)
XLA Ops:
  0.6 50.4 %winds.1 = (bf16[2,2,22,8,128]{4,3,2,1,0:T(8,128)(2,1)}, f32[2,2,176,128]{3,2,1,0:T(8,128)}) custom-call(bf16[2,5,8,641]{3,2,1,0:T(8,128)(2,1)} %bitcast.22, bf16[5,64,641]{2,1,0:T(8,128)(2,1)} %bitcast.21, s32[5]{0:T(128)} %pair_ref.1, bf16[2,640,1408]{2,1,0:T(8,128)(2,1)} %constant.2.clone.basis_ref, bf16[2,22,8,128]{3,2,1,0:T(8,128)(2,1)} %bitcast.23, ...), custom_call_target="tpu_custom_call" | custom-call | tf_op jit(solution)/shard_map/winds/pallas_call | solution.py:633
  51.0 1.9 %results.1 = (bf16[2,2,22,8,128]{4,3,2,1,0:T(8,128)(2,1)}, f32[2,2,176,128]{3,2,1,0:T(8,128)}) custom-call(bf16[2,2,22,8,128]{4,3,2,1,0:T(8,128)(2,1)} %get-tuple-element.6.adv_ref, f32[2,2,176,128]{3,2,1,0:T(8,128)} %get-tuple-element.7.disp_ref), custom_call_target="tpu_custom_call" | custom-call | tf_op jit(solution)/shard_map/results/pallas_call | solution.py:691

commit v5 on v4

--- a/solution.py
+++ b/solution.py
@@ -16,7 +16,7 @@
 F32 = jnp.float32
 TAP = jnp.bfloat16
 VMEM_LIMIT = 60 * 1024 * 1024
-GROUPS = 8
+GROUPS = 16
 
 
 def nt_dot(a, b):
@@ -337,7 +337,7 @@
     halo,
     *rest,
 ):
-    qp = grid.shape[0] // 8 * 8 // 288
+    qp = grid.shape[0] // 289
     half = nb * pairs // 2
     window = place.shape[1] // 2
     lon_half = nq * 64
@@ -645,14 +645,14 @@
             pltpu.VMEM((144, 8, 2 * window), F32),
             pltpu.VMEM((2, 4, 288, window), BF16),
             pltpu.VMEM(basis.shape, BF16),
-            pltpu.VMEM((288 * qp + 8, 128), F32),
+            pltpu.VMEM((289 * qp, 128), F32),
             pltpu.VMEM((12, 6, qp // 8, 2, 5, 16, 128), TAP),
             pltpu.VMEM(eta.shape, BF16),
             pltpu.VMEM(cells.shape, jnp.int32),
             pltpu.VMEM((8, 4, 2 * qp, 128), F32),
             pltpu.VMEM((nq * 8, 128), F32),
-            pltpu.VMEM((2, 2, qp * 8, 128), F32),
-            pltpu.VMEM((2, 2, qp * 8, 128), F32),
+            pltpu.VMEM((2, 2, qp * 8 + 8, 128), F32),
+            pltpu.VMEM((2, 2, qp * 8 + 8, 128), F32),
             pltpu.VMEM((2, 2, qp, 8, 128), BF16),
             dma((-(-lon_total // 512),)),
             dma((2,)),

time: 53.1 us -> 53 us (level)
  no operation moved by 1% of the time
where the time goes in v5:
time: 53 us; the launch traced here: 52.8 us
  Pallas kernels  52.1 us (98%)
  between operations  0.64 us (1%)
    pallas_call x1, Pallas kernels, per_device(): pl.pallas_call(functools.partial(whole_kernel, nb, nx, nq, pairs, width),...  50.3 us
    pallas_call x1, Pallas kernels, per_device(): pl.pallas_call(hand_over, out_shape=(jax.ShapeDtypeStruct(adv.shape, adv....  1.85 us

profile of v5, /device:TPU:1, one launch (start us, length us, event | category | flops | bytes accessed | tf_op | source)
XLA Modules:
  0.0 52.8 jit_solution(17888611538329327829)
XLA Ops:
  0.6 50.3 %winds.1 = (bf16[2,2,22,8,128]{4,3,2,1,0:T(8,128)(2,1)}, f32[2,2,176,128]{3,2,1,0:T(8,128)}) custom-call(bf16[2,5,8,641]{3,2,1,0:T(8,128)(2,1)} %bitcast.22, bf16[5,64,641]{2,1,0:T(8,128)(2,1)} %bitcast.21, s32[5]{0:T(128)} %pair_ref.1, bf16[2,640,1408]{2,1,0:T(8,128)(2,1)} %constant.2.clone.basis_ref, bf16[2,22,8,128]{3,2,1,0:T(8,128)(2,1)} %bitcast.23, ...), custom_call_target="tpu_custom_call" | custom-call | tf_op jit(solution)/shard_map/winds/pallas_call | solution.py:633
  50.9 1.9 %results.1 = (bf16[2,2,22,8,128]{4,3,2,1,0:T(8,128)(2,1)}, f32[2,2,176,128]{3,2,1,0:T(8,128)}) custom-call(bf16[2,2,22,8,128]{4,3,2,1,0:T(8,128)(2,1)} %get-tuple-element.6.adv_ref, f32[2,2,176,128]{3,2,1,0:T(8,128)} %get-tuple-element.7.disp_ref), custom_call_target="tpu_custom_call" | custom-call | tf_op jit(solution)/shard_map/results/pallas_call | solution.py:691
